TPU v7x, 128 devices: a whole 4x4x4 slice. The times are simulated.
128 devices in a mesh: tok: 16 (over y, x), exp: 8 (over z, core).
Axes of the slice: x: 4, y: 4, z: 4, core: 2. Of those that a mesh axis runs over, the one named last changes fastest.
Arguments:
- x_var: bfloat16 [48, 16, 1024, 1024], P('tok', None, 'exp'), may hold values from -40 to 40
- var_ids: int32 [48], P('tok'), may hold values from 0 to 47, each once
- var_embed: bfloat16 [48, 1024], replicated, may hold values from -3 to 3
- score_vecs: bfloat16 [1024, 16], replicated, may hold values from -0.1875 to 0.1875
- v_weight: bfloat16 [1024, 1024], replicated, may hold values from -0.1875 to 0.1875
- out_weight: bfloat16 [1024, 1024], replicated, may hold values from -0.1875 to 0.1875
- second_half: bfloat16 [16384, 1024], P(('tok', 'exp')), may hold values from -6 to 6
- norm_gain: bfloat16 [1024], replicated, may hold values from 0.099609375 to 1.8984375
- routes: int32 [16384, 2], P(('tok', 'exp')), may hold values from 0 to 63, all different within a row; in each aligned block of 128 rows (0 to 127, 128 to 255, ...) at most 7 rows name the same one
- route_weights: float32 [16384, 2], P(('tok', 'exp')), may hold values from 0.2 to 1
- w_gate: bfloat16 [64, 1024, 2048], P('tok', None, 'exp'), may hold values from -0.1875 to 0.1875
- w_up: bfloat16 [64, 1024, 2048], P('tok', None, 'exp'), may hold values from -0.1875 to 0.1875
- w_down: bfloat16 [64, 2048, 1024], P('tok', 'exp'), may hold values from -0.125 to 0.125
Outputs:
- blended: bfloat16 [16384, 1024], P(('tok', 'exp'))
Inputs may be any that keep to these rules, and one draw needn't show every extreme that they name: `routes`: in the rows of one device no expert is named more than 7 times, and in some device some expert is named exactly 7 times; every token names two different experts.
All inputs are finite; a program needn't handle non-finite values.
Results may differ from a plain program's by a relative error of at most 0.018.
Values may be sent and summed in bfloat16 or wider, within the bound.
A program may use at most 192 MiB of HBM per device.

v0:
```python
import jax
import jax.numpy as jnp
from jax import lax
from jax.sharding import PartitionSpec as P

EXPERTS = 64
CAP = 7


def add_labels(x_var, var_ids, var_embed):
    count = var_embed.shape[0]
    picks = (var_ids[:, None] == jnp.arange(count, dtype=jnp.int32)[None, :]).astype(jnp.bfloat16)
    labels = jnp.dot(picks, var_embed, preferred_element_type=jnp.float32)
    shaped = labels.reshape((labels.shape[0], 1, 1, labels.shape[1]))
    return (x_var.astype(jnp.float32) + shaped).astype(jnp.bfloat16)


def project_heads(mixture, value_heads):
    return jnp.einsum("thd,dhj->thj", mixture, value_heads, precision=lax.Precision.HIGHEST)


def aggregate(x_var, var_ids, var_embed, score_vecs, v_weight, out_weight):
    width = x_var.shape[3]
    heads_count = score_vecs.shape[1]
    value_heads = v_weight.astype(jnp.float32).reshape(width, heads_count, width // heads_count)
    embedded = add_labels(x_var, var_ids, var_embed)
    whole = lax.all_to_all(embedded, "tok", split_axis=1, concat_axis=0, tiled=True)
    whole = whole.reshape(whole.shape[0], whole.shape[2], whole.shape[3])
    scores = jnp.einsum("vtd,dh->vth", whole, score_vecs, preferred_element_type=jnp.float32)
    peak = jnp.max(scores, axis=0)
    expo = jnp.exp(scores - peak[None])
    denom = jnp.sum(expo, axis=0)
    attn_weights = expo.astype(jnp.bfloat16)
    mixture = jnp.einsum("vth,vtd->thd", attn_weights, whole, preferred_element_type=jnp.float32)
    heads = project_heads(mixture, value_heads) / denom[..., None]
    heads = heads.reshape(heads.shape[0], width)
    return jnp.dot(heads.astype(jnp.bfloat16), out_weight, preferred_element_type=jnp.float32)


def experts_path(second_half, norm_gain, routes, route_weights, w_gate, w_up, w_down):
    tok_rows, width = second_half.shape
    level = second_half.astype(jnp.float32)
    scale = lax.rsqrt(jnp.mean(level * level, axis=-1, keepdims=True) + 1e-06)
    normed = (level * scale * norm_gain.astype(jnp.float32)).astype(jnp.bfloat16)
    flat_ids = routes.reshape(-1)
    picks = (flat_ids[:, None] == jnp.arange(EXPERTS, dtype=jnp.int32)[None, :]).astype(jnp.int32)
    earlier = jnp.cumsum(picks, axis=0) - picks
    slots = jnp.sum(earlier * picks, axis=1)
    target = flat_ids * CAP + slots
    repeated = jnp.repeat(normed, 2, axis=0)
    placing = (target[None, :] == jnp.arange(EXPERTS * CAP, dtype=jnp.int32)[:, None]).astype(
        jnp.bfloat16
    )
    packed = jnp.dot(placing, repeated, preferred_element_type=jnp.float32).astype(jnp.bfloat16)
    groups = lax.axis_size("tok")
    packed = packed.reshape(groups, EXPERTS // groups, CAP, width)
    arrived = lax.all_to_all(packed, "tok", split_axis=0, concat_axis=0, tiled=True)
    piece = lax.all_gather(arrived, "exp", axis=0, tiled=True)
    gate = jnp.einsum("secd,edf->secf", piece, w_gate, preferred_element_type=jnp.float32)
    up = jnp.einsum("secd,edf->secf", piece, w_up, preferred_element_type=jnp.float32)
    hidden = (jax.nn.silu(gate) * up).astype(jnp.bfloat16)
    partial_out = jnp.einsum("secf,efd->secd", hidden, w_down, preferred_element_type=jnp.float32)
    summed = lax.psum_scatter(
        partial_out.astype(jnp.bfloat16), "exp", scatter_dimension=0, tiled=True
    )
    returned = lax.all_to_all(summed, "tok", split_axis=0, concat_axis=0, tiled=True)
    results = returned.reshape(EXPERTS * CAP, width)
    picked = jnp.take(results, target, axis=0).reshape(tok_rows, 2, width).astype(jnp.float32)
    return jnp.sum(picked * route_weights[..., None], axis=1)


def shards(
    x_var,
    var_ids,
    var_embed,
    score_vecs,
    v_weight,
    out_weight,
    second_half,
    norm_gain,
    routes,
    route_weights,
    w_gate,
    w_up,
    w_down,
):
    cross = aggregate(x_var, var_ids, var_embed, score_vecs, v_weight, out_weight)
    moe = experts_path(second_half, norm_gain, routes, route_weights, w_gate, w_up, w_down)
    return (cross + moe).astype(jnp.bfloat16)


def solution(mesh):
    in_specs = (
        P("tok", None, "exp", None),
        P("tok"),
        P(),
        P(),
        P(),
        P(),
        P(("tok", "exp"), None),
        P(),
        P(("tok", "exp"), None),
        P(("tok", "exp"), None),
        P("tok", None, "exp"),
        P("tok", None, "exp"),
        P("tok", "exp", None),
    )
    out_specs = P(("tok", "exp"), None)
    return jax.shard_map(shards, mesh=mesh, in_specs=in_specs, out_specs=out_specs, check_vma=False)
```

profile of v0, /device:TPU:0, one launch (start us, length us, event | category | flops | bytes accessed | tf_op | source)
XLA Modules:
  0.0 368.8 jit_solution(9763495825705794042)
XLA Ops:
  6.5 0.9 copy.59
  7.8 0.6 reduce-window.6
  8.7 0.7 convert_element_type.60
  9.4 1.1 fusion.29
  10.5 1.1 fusion.31
  12.1 1.3 convolution_convert_fusion
  13.4 1.4 reshape.108
  14.8 0.9 copy.64
  15.7 22.7 %all_to_all.25 = bf16[16,4,7,1024]{3,1,2,0:T(4,128)(2,1)S(1)} all-to-all(bf16[16,4,7,1024]{3,1,2,0:T(4,128)(2,1)S(1)} %copy.64), channel_id=1, replica_groups=mesh['tok'=16,'exp'=8] {'tok'}, dimensions={0} | all-to-all | bytes 1835008 | tf_op jit(solution)/shard_map/all_to_all | solution.py:57
  38.4 1.2 copy.65
  39.6 44.0 %all-gather.2.cloned.1.call-done = bf16[128,4,7,1024]{3,0,2,1:T(8,128)(2,1)} async-done(((bf16[16,4,7,1024]{3,0,2,1:T(8,128)(2,1)}), bf16[128,4,7,1024]{3,0,2,1:T(8,128)(2,1)}) %all-gather.2.cloned.1.call-update) | async-done | bytes 7340048 | tf_op jit(solution)/shard_map/all_gather | solution.py:58
  83.7 7.6 %fusion.9 = f32[4,128,7,256]{3,1,2,0:T(8,128)} fusion(bf16[128,4,7,1024]{3,0,2,1:T(8,128)(2,1)} %all-gather.2.cloned.1.call-done, bf16[4,1024,256]{2,1,0:T(8,128)(2,1)} %param.24), kind=kOutput, calls=%fused_computation.15 | convolution fusion | flops 1879048192 | bytes 13107200 | tf_op jit(solution)/shard_map/secd,edf->secf/dot_general | solution.py:60
  91.3 9.4 %convert_bitcast_fusion = bf16[128,4,7,1024]{3,0,2,1:T(8,128)(2,1)} fusion(bf16[4,256,1024]{2,1,0:T(8,128)(2,1)S(1)} %copy-done, f32[4,128,7,256]{3,1,2,0:T(8,128)} %fusion.9, bf16[128,4,7,1024]{3,0,2,1:T(8,128)(2,1)} %all-gather.2.cloned.1.call-done, bf16[4,1024,256]{2,1,0:T(8,128)(2,1)} %param.23), kind=kOutput, calls=%fused_computation.6 | convolution fusion | flops 3767271424 | bytes 22544384 | tf_op jit(solution)/shard_map/secf,efd->secd/dot_general | solution.py:62
  100.7 0.9 copy-done.6
  101.8 11.5 %add_convert_fusion = bf16[3,16,128,1024]{3,2,0,1:T(8,128)(2,1)} fusion(bf16[3,16,128,1024]{3,2,1,0:T(8,128)(2,1)} %param.13, f32[3,1024]{1,0:T(4,128)S(1)} %fusion.41), kind=kLoop, calls=%fused_computation.1 | loop fusion | flops 18874368 | bytes 25178112 | tf_op jit(solution)/shard_map/convert_element_type | solution.py:15
  113.3 7.0 %all-to-all-start = ((bf16[3,16,128,1024]{3,2,0,1:T(8,128)(2,1)}), bf16[3,16,128,1024]{3,2,0,1:T(8,128)(2,1)}, u32[]{:S(2)}, u32[]{:S(2)}) async-start(bf16[3,16,128,1024]{3,2,0,1:T(8,128)(2,1)} %add_convert_fusion), calls=%async_computation | async-start | bytes 25165824 | tf_op jit(solution)/shard_map/all_to_all | solution.py:27
  121.0 0.7 copy.69
  121.8 2.9 copy.57
  124.7 0.6 pad_clamp_fusion
  125.3 183.8 %all-to-all-done = bf16[3,16,128,1024]{3,2,0,1:T(8,128)(2,1)} async-done(((bf16[3,16,128,1024]{3,2,0,1:T(8,128)(2,1)}), bf16[3,16,128,1024]{3,2,0,1:T(8,128)(2,1)}, u32[]{:S(2)}, u32[]{:S(2)}) %all-to-all-start) | async-done | bytes 12582944 | tf_op jit(solution)/shard_map/all_to_all | solution.py:27
  309.1 6.3 %fusion.44 = (f32[128,16]{0,1:T(8,128)S(1)}, f32[48,128,16]{1,2,0:T(8,128)S(1)}) fusion(bf16[48,128,1024]{2,1,0:T(8,128)(2,1)} %bitcast.2, bf16[1024,16]{0,1:T(8,128)(2,1)S(1)} %copy-done.2), kind=kOutput, calls=%fused_computation.60 | convolution fusion | flops 201422848 | bytes 13017088 | tf_op jit(solution)/shard_map/vtd,dh->vth/dot_general | solution.py:29
  315.4 0.7 fusion.32
  316.1 0.5 copy.55
  316.7 2.9 copy.66
  319.5 3.8 %all-to-all-start.2 = ((bf16[16,4,7,1024]{3,1,2,0:T(4,128)(2,1)}), bf16[16,4,7,1024]{3,1,2,0:T(4,128)(2,1)S(1)}, u32[]{:S(2)}, u32[]{:S(2)}) async-start(bf16[16,4,7,1024]{3,1,2,0:T(4,128)(2,1)} %copy.66), calls=%async_computation.3 | async-start | bytes 1835008 | tf_op jit(solution)/shard_map/all_to_all | solution.py:66
  323.4 20.7 %fusion = f32[128,16,1024]{2,1,0:T(8,128)S(1)} fusion(bf16[48,128,16]{0,2,1:T(8,128)(2,1)S(1)} %copy.55, bf16[48,128,1024]{2,1,0:T(8,128)(2,1)} %bitcast.2), kind=kOutput, calls=%fused_computation.2 | convolution fusion | flops 201326592 | bytes 21168128 | tf_op jit(solution)/shard_map/vth,vtd->thd/dot_general | solution.py:34
  344.1 10.1 %fusion.22 = bf16[128,16,64]{0,2,1:T(8,128)(2,1)} fusion(bf16[1024,16,64]{0,2,1:T(8,128)(2,1)S(1)} %bitcast.88, f32[128,16,1024]{2,1,0:T(8,128)S(1)} %fusion, f32[128,16]{0,1:T(8,128)S(1)} %copy-done.3), kind=kOutput, calls=%fused_computation.27 | convolution fusion | flops 1610874880 | bytes 10756096 | tf_op jit(solution)/shard_map/thd,dhj->thj/dot_general | solution.py:19
  354.2 0.4 copy.67
  354.5 0.3 reshape.109
  354.9 1.4 gather_fusion
  356.5 2.5 multiply_reduce_fusion
  359.1 2.9 fusion.18
  (42 shorter events, 2.2 us)
Async XLA Ops:
  6.5 84.8 %copy-start = (bf16[4,256,1024]{2,1,0:T(8,128)(2,1)S(1)}, bf16[4,256,1024]{2,1,0:T(8,128)(2,1)}, u32[]{:S(2)}) copy-start(bf16[4,256,1024]{2,1,0:T(8,128)(2,1)} %param.25) | copy-start | bytes 6291460
  6.5 77.1 %all-gather.2.cloned.1.call-start = ((), (), s32[]{:S(2)}) async-start(), calls=%async_computation.4 | async-start | bytes 8257536 | tf_op jit(solution)/shard_map/all_gather | solution.py:58
  39.6 277.1 %reduce-scatter.2.cloned.1.call-start = ((), (), s32[]{:S(2)}) async-start(), calls=%async_computation.5 | async-start | bytes 8257536 | tf_op jit(solution)/shard_map/reduce_scatter | solution.py:63
  100.7 0.9 copy-start.6
  100.7 0.9 copy-start.7
  113.3 7.2 %copy-start.4 = (s32[128,2]{0,1:T(2,128)S(1)}, s32[128,2]{0,1:T(2,128)}, u32[]{:S(2)}) copy-start(s32[128,2]{0,1:T(2,128)} %param.21) | copy-start | bytes 3076
  113.3 7.7 %copy-start.5 = (f32[128,2]{0,1:T(2,128)S(1)}, f32[128,2]{0,1:T(2,128)}, u32[]{:S(2)}) copy-start(f32[128,2]{0,1:T(2,128)} %param.22) | copy-start | bytes 3076
  113.3 195.8 %all-to-all-start = ((bf16[3,16,128,1024]{3,2,0,1:T(8,128)(2,1)}), bf16[3,16,128,1024]{3,2,0,1:T(8,128)(2,1)}, u32[]{:S(2)}, u32[]{:S(2)}) async-start(bf16[3,16,128,1024]{3,2,0,1:T(8,128)(2,1)} %add_convert_fusion), calls=%async_computation | async-start | bytes 25165824 | tf_op jit(solution)/shard_map/all_to_all | solution.py:27
  120.3 188.7 %copy-start.2 = (bf16[1024,16]{0,1:T(8,128)(2,1)S(1)}, bf16[1024,16]{0,1:T(8,128)(2,1)}, u32[]{:S(2)}) copy-start(bf16[1024,16]{0,1:T(8,128)(2,1)} %param.16) | copy-start | bytes 98308
  319.5 34.6 %all-to-all-start.2 = ((bf16[16,4,7,1024]{3,1,2,0:T(4,128)(2,1)}), bf16[16,4,7,1024]{3,1,2,0:T(4,128)(2,1)S(1)}, u32[]{:S(2)}, u32[]{:S(2)}) async-start(bf16[16,4,7,1024]{3,1,2,0:T(4,128)(2,1)} %copy.66), calls=%async_computation.3 | async-start | bytes 1835008 | tf_op jit(solution)/shard_map/all_to_all | solution.py:66
  323.4 20.7 %copy-start.3 = (f32[128,16]{0,1:T(8,128)S(1)}, f32[128,16]{0,1:T(8,128)}, u32[]{:S(2)}) copy-start(f32[128,16]{0,1:T(8,128)} %get-tuple-element.5) | copy-start | bytes 24580
  354.9 7.1 %copy-start.1 = (bf16[4,256,1024]{2,1,0:T(8,128)(2,1)S(1)}, bf16[4,256,1024]{2,1,0:T(8,128)(2,1)}, u32[]{:S(2)}) copy-start(bf16[4,256,1024]{2,1,0:T(8,128)(2,1)} %param.25) | copy-start | bytes 6291460
Sparse Core Ops, SparseCore 0:
  39.7 43.9 all-gather.1
  100.9 47.6 reduce-scatter.1
where the time goes:
time: 370 us; the launch traced here: 369 us
  waiting for transfers between devices  228 us (62%)
  matrix products  58.5 us (16%)
  blocking collectives  22.7 us (6%)
  other arithmetic  19 us (5%)
  local copies, waits for them, and re-layouts  16.1 us (4%)
  between operations  13.6 us (4%)
  starting transfers between devices  10.9 us (3%)
    all_to_all x1, waiting for transfers between devices, aggregate(): lax.all_to_all(embedded, 'tok', split_axis=1, concat_axis=0, tiled=True)  184 us
    all_gather x1, waiting for transfers between devices, experts_path(): piece = lax.all_gather(arrived, 'exp', axis=0, tiled=True)  44 us
    all_to_all x1, blocking collectives, experts_path(): lax.all_to_all(packed, 'tok', split_axis=0, concat_axis=0, tiled=True)  22.7 us
    dot_general x1, matrix products, aggregate(): jnp.einsum('vth,vtd->thd', attn_weights, whole, preferred_element_type=jn...  20.7 us
    convert_element_type x1, other arithmetic, add_labels(): return (x_var.astype(jnp.float32) + shaped).astype(jnp.bfloat16)  11.5 us
    dot_general x1, matrix products, project_heads(): jnp.einsum('thd,dhj->thj', mixture, value_heads, precision=lax.Precision....  10.1 us
    dot_general x1, matrix products, experts_path(): jnp.einsum('secf,efd->secd', hidden, w_down, preferred_element_type=jnp.f...  9.37 us
    dot_general x1, matrix products, experts_path(): jnp.einsum('secd,edf->secf', piece, w_up, preferred_element_type=jnp.floa...  7.65 us
  transfers between devices with their start and end apart: 4, of which 2 were waited for; matrix products, arithmetic and copies ran while one was open for 15% of the time, Pallas kernels for 0%

commit v1 on v0

--- a/solution.py
+++ b/solution.py
@@ -15,26 +15,30 @@
     return (x_var.astype(jnp.float32) + shaped).astype(jnp.bfloat16)
 
 
-def project_heads(mixture, value_heads):
-    return jnp.einsum("thd,dhj->thj", mixture, value_heads, precision=lax.Precision.HIGHEST)
-
-
 def aggregate(x_var, var_ids, var_embed, score_vecs, v_weight, out_weight):
     width = x_var.shape[3]
     heads_count = score_vecs.shape[1]
-    value_heads = v_weight.astype(jnp.float32).reshape(width, heads_count, width // heads_count)
     embedded = add_labels(x_var, var_ids, var_embed)
-    whole = lax.all_to_all(embedded, "tok", split_axis=1, concat_axis=0, tiled=True)
-    whole = whole.reshape(whole.shape[0], whole.shape[2], whole.shape[3])
-    scores = jnp.einsum("vtd,dh->vth", whole, score_vecs, preferred_element_type=jnp.float32)
-    peak = jnp.max(scores, axis=0)
+    scores = jnp.einsum("vntd,dh->vnth", embedded, score_vecs, preferred_element_type=jnp.float32)
+    peak = lax.pmax(jnp.max(scores, axis=0), "tok")
+    values = jnp.einsum(
+        "vntd,dk->vntk", embedded, v_weight, preferred_element_type=jnp.float32
+    ).astype(jnp.bfloat16)
     expo = jnp.exp(scores - peak[None])
-    denom = jnp.sum(expo, axis=0)
-    attn_weights = expo.astype(jnp.bfloat16)
-    mixture = jnp.einsum("vth,vtd->thd", attn_weights, whole, preferred_element_type=jnp.float32)
-    heads = project_heads(mixture, value_heads) / denom[..., None]
-    heads = heads.reshape(heads.shape[0], width)
-    return jnp.dot(heads.astype(jnp.bfloat16), out_weight, preferred_element_type=jnp.float32)
+    denom = lax.psum_scatter(jnp.sum(expo, axis=0), "tok", scatter_dimension=0, tiled=True)
+    spread = (
+        jnp.arange(heads_count)[:, None] == jnp.arange(width)[None, :] // (width // heads_count)
+    ).astype(jnp.bfloat16)
+    weights = jnp.einsum(
+        "vnth,hk->vntk", expo.astype(jnp.bfloat16), spread, preferred_element_type=jnp.float32
+    ).astype(jnp.bfloat16)
+    mixed = jnp.sum(weights.astype(jnp.float32) * values.astype(jnp.float32), axis=0)
+    mixed = lax.psum_scatter(
+        mixed.astype(jnp.bfloat16), "tok", scatter_dimension=0, tiled=True
+    )[0].astype(jnp.float32)
+    inverse = jnp.repeat(1.0 / denom[0], width // heads_count, axis=1)
+    heads = (mixed * inverse).astype(jnp.bfloat16)
+    return jnp.dot(heads, out_weight, preferred_element_type=jnp.float32)
 
 
 def experts_path(second_half, norm_gain, routes, route_weights, w_gate, w_up, w_down):

time: 370 us -> 271 us (0.73)
  waiting for transfers between devices: 228 us -> 134 us
  other arithmetic: 19 us -> 11.4 us
  starting transfers between devices: 10.9 us -> 5.38 us
  local copies, waits for them, and re-layouts: 16.1 us -> 21 us
    all_to_all x1 -> x0, waiting for transfers between devices: 184 us -> none  [aggregate(): lax.all_to_all(embedded, 'tok', split_axis=1, concat_axis=0, tiled=True)]
    unnamed x2 -> x7, waiting for transfers between devices: 0.03 us -> 71.4 us
    pmax x0 -> x1, waiting for transfers between devices: none -> 26.3 us  [aggregate(): peak = lax.pmax(jnp.max(scores, axis=0), 'tok')]
    convert_element_type x1, other arithmetic: 11.5 us -> 1.72 us  [aggregate(): heads = (mixed * inverse).astype(jnp.bfloat16)]
    all_gather x1, waiting for transfers between devices: 44 us -> 36.7 us  [experts_path(): piece = lax.all_gather(arrived, 'exp', axis=0, tiled=True)]
    all_to_all x1 -> x0, starting transfers between devices: 7.03 us -> none  [aggregate(): lax.all_to_all(embedded, 'tok', split_axis=1, concat_axis=0, tiled=True)]
    convert_element_type x1, local copies, waits for them, and re-layouts: 0.5 us -> 6.39 us  [aggregate(): mixed.astype(jnp.bfloat16)]
  transfers between devices with their start and end apart: 4 -> 6, of which waited for: 2 -> 4; matrix products, arithmetic and copies ran while one was open for 15% -> 27% of each run, Pallas kernels for 0% -> 0%
where the time goes in v1:
time: 271 us
  waiting for transfers between devices  134 us (49%)
  matrix products  61 us (23%)
  blocking collectives  22.7 us (8%)
  local copies, waits for them, and re-layouts  21 us (8%)
  between operations  14.8 us (5%)
  other arithmetic  11.4 us (4%)
  starting transfers between devices  5.38 us (2%)
    unnamed x7, waiting for transfers between devices  71.4 us
    all_gather x1, waiting for transfers between devices, experts_path(): piece = lax.all_gather(arrived, 'exp', axis=0, tiled=True)  36.7 us
    pmax x1, waiting for transfers between devices, aggregate(): peak = lax.pmax(jnp.max(scores, axis=0), 'tok')  26.3 us
    dot_general x1, matrix products, aggregate(): jnp.einsum('vntd,dk->vntk', embedded, v_weight, preferred_element_type=jn...  25.1 us
    all_to_all x1, blocking collectives, experts_path(): lax.all_to_all(packed, 'tok', split_axis=0, concat_axis=0, tiled=True)  22.7 us
    dot_general x1, matrix products, experts_path(): jnp.einsum('secf,efd->secd', hidden, w_down, preferred_element_type=jnp.f...  9.38 us
    dot_general x1, matrix products, experts_path(): jnp.einsum('secd,edf->secf', piece, w_up, preferred_element_type=jnp.floa...  7.67 us
    dot_general x1, matrix products, aggregate(): jnp.einsum('vnth,hk->vntk', expo.astype(jnp.bfloat16), spread, preferred_...  7.49 us
  transfers between devices with their start and end apart: 6, of which 4 were waited for; matrix products, arithmetic and copies ran while one was open for 27% of the time, Pallas kernels for 0%

profile of v1, /device:TPU:0, one launch (start us, length us, event | category | flops | bytes accessed | tf_op | source)
XLA Modules:
  0.0 270.7 jit_solution(11365542898626623314)
XLA Ops:
  7.4 0.9 copy.43
  8.6 0.6 reduce-window.6
  9.6 0.7 convert_element_type.84
  10.3 1.1 fusion.19
  11.3 1.1 fusion.21
  12.9 1.3 convolution_convert_fusion
  14.3 1.4 reshape.141
  15.7 0.9 copy.48
  16.6 22.7 %all_to_all.10 = bf16[16,4,7,1024]{3,1,2,0:T(4,128)(2,1)S(1)} all-to-all(bf16[16,4,7,1024]{3,1,2,0:T(4,128)(2,1)S(1)} %copy.48), channel_id=1, replica_groups=mesh['tok'=16,'exp'=8] {'tok'}, dimensions={0} | all-to-all | bytes 1835008 | tf_op jit(solution)/shard_map/all_to_all | solution.py:61
  39.2 1.2 copy.49
  40.7 7.0 %fusion.44 = (f32[16,128,16]{1,2,0:T(8,128)}, f32[3,16,128,16]{2,3,1,0:T(8,128)S(1)}) fusion(bf16[1024,16]{0,1:T(8,128)(2,1)S(1)} %copy-done.6, bf16[3,16,128,1024]{3,2,1,0:T(8,128)(2,1)} %param.13, f32[3,1024]{1,0:T(4,128)S(1)} %fusion.41), kind=kOutput, calls=%fused_computation.72 | convolution fusion | flops 220266496 | bytes 13152256 | tf_op jit(solution)/shard_map/vntd,dh->vnth/dot_general | solution.py:22
  47.8 36.7 %all-gather.2.cloned.1.call-done = bf16[128,4,7,1024]{3,0,2,1:T(8,128)(2,1)} async-done(((bf16[16,4,7,1024]{3,0,2,1:T(8,128)(2,1)}), bf16[128,4,7,1024]{3,0,2,1:T(8,128)(2,1)}) %all-gather.2.cloned.1.call-update) | async-done | bytes 7340048 | tf_op jit(solution)/shard_map/all_gather | solution.py:62
  84.6 7.7 %fusion.7 = f32[4,128,7,256]{3,1,2,0:T(8,128)} fusion(bf16[128,4,7,1024]{3,0,2,1:T(8,128)(2,1)} %all-gather.2.cloned.1.call-done, bf16[4,1024,256]{2,1,0:T(8,128)(2,1)} %param.24), kind=kOutput, calls=%fused_computation.14 | convolution fusion | flops 1879048192 | bytes 13107200 | tf_op jit(solution)/shard_map/secd,edf->secf/dot_general | solution.py:64
  92.2 9.4 %convert_bitcast_fusion = bf16[128,4,7,1024]{3,0,2,1:T(8,128)(2,1)} fusion(bf16[4,256,1024]{2,1,0:T(8,128)(2,1)S(1)} %copy-done, f32[4,128,7,256]{3,1,2,0:T(8,128)} %fusion.7, bf16[128,4,7,1024]{3,0,2,1:T(8,128)(2,1)} %all-gather.2.cloned.1.call-done, bf16[4,1024,256]{2,1,0:T(8,128)(2,1)} %param.23), kind=kOutput, calls=%fused_computation.5 | convolution fusion | flops 3767271424 | bytes 22544384 | tf_op jit(solution)/shard_map/secf,efd->secd/dot_general | solution.py:66
  101.7 26.3 %all-reduce.5.cloned.1.call-done = f32[16,128,16]{1,2,0:T(8,128)} async-done(((f32[16,128,16]{1,2,0:T(8,128)}), f32[16,128,16]{1,2,0:T(8,128)}) %all-reduce.5.cloned.1.call-update) | async-done | bytes 131088 | tf_op jit(solution)/shard_map/pmax | solution.py:23
  128.0 1.6 fusion.23
  129.9 7.5 %fusion.26 = bf16[3,16,128,1024]{3,2,1,0:T(8,128)(2,1)} fusion(f32[3,16,128,16]{2,3,1,0:T(8,128)S(1)} %get-tuple-element.6, f32[16,128,16]{1,2,0:T(8,128)} %all-reduce.5.cloned.1.call-done, s32[1024]{0:T(1024)S(1)} %add_select_fusion), kind=kOutput, calls=%fused_computation.37 | convolution fusion | flops 201539584 | bytes 13111296 | tf_op jit(solution)/shard_map/vnth,hk->vntk/dot_general | solution.py:32
  137.4 25.1 %multiply_reduce_fusion = bf16[16,128,1024]{2,1,0:T(8,128)(2,1)} fusion(bf16[3,16,128,1024]{3,2,1,0:T(8,128)(2,1)} %fusion.26, bf16[3,16,128,1024]{3,2,1,0:T(8,128)(2,1)} %param.13, f32[3,1024]{1,0:T(4,128)S(1)} %fusion.41, bf16[1024,1024]{1,0:T(8,128)(2,1)S(1)} %copy-done.4), kind=kOutput, calls=%fused_computation.1 | convolution fusion | flops 12933136384 | bytes 31469568 | tf_op jit(solution)/shard_map/vntd,dk->vntk/dot_general | solution.py:24
  162.5 6.4 %copy.42 = bf16[16,128,1024]{1,2,0:T(8,128)(2,1)} copy(bf16[16,128,1024]{2,1,0:T(8,128)(2,1)} %multiply_reduce_fusion) | data formatting | bytes 8388608 | tf_op jit(solution)/shard_map/convert_element_type | solution.py:37
  169.1 2.8 %copy.50 = bf16[16,4,7,1024]{3,1,2,0:T(4,128)(2,1)} copy(bf16[16,4,7,1024]{3,0,2,1:T(8,128)(2,1)} %reduce-scatter.5.cloned.1.call-done) | data formatting | bytes 1835008 | tf_op jit(solution)/shard_map/reduce_scatter | solution.py:67
  171.9 5.0 %all-to-all-start.1 = ((bf16[16,4,7,1024]{3,1,2,0:T(4,128)(2,1)}), bf16[16,4,7,1024]{3,1,2,0:T(4,128)(2,1)S(1)}, u32[]{:S(2)}, u32[]{:S(2)}) async-start(bf16[16,4,7,1024]{3,1,2,0:T(4,128)(2,1)} %copy.50), calls=%async_computation.2 | async-start | bytes 1835008 | tf_op jit(solution)/shard_map/all_to_all | solution.py:70
  177.5 0.7 copy.53
  178.8 0.6 pad_clamp_fusion
  179.4 39.3 %all-reduce.7.cloned.1.call-done = f32[16,128,16]{1,2,0:T(8,128)} async-done(((f32[16,128,16]{1,2,0:T(8,128)}), f32[16,128,16]{1,2,0:T(8,128)}) %all-reduce.7.cloned.1.call-update) | async-done | bytes 131088
  218.7 1.3 fusion.37
  220.0 32.0 %reduce-scatter.7.cloned.1.call-done = bf16[1,128,1024]{1,2,0:T(8,128)(2,1)} async-done(((bf16[16,128,1024]{1,2,0:T(8,128)(2,1)}), bf16[1,128,1024]{1,2,0:T(8,128)(2,1)}) %reduce-scatter.7.cloned.1.call-update) | async-done | bytes 262160
  252.0 1.7 fusion.22
  253.7 1.3 copy.51
  255.0 1.6 reshape.142
  256.6 1.3 gather_fusion
  258.1 2.5 multiply_reduce_fusion.1
  260.7 2.9 %fusion.14 = bf16[128,1024]{1,0:T(8,128)(2,1)} fusion(f32[128,1024]{1,0:T(8,128)S(1)} %multiply_reduce_fusion.1, bf16[128,1024]{0,1:T(8,128)(2,1)} %fusion.22, bf16[1024,1024]{1,0:T(8,128)(2,1)} %param.18), kind=kOutput, calls=%fused_computation.22 | convolution fusion | flops 268697600 | bytes 3145728 | tf_op jit(solution)/shard_map/dot_general | solution.py:41
  (53 shorter events, 3.2 us)
Async XLA Ops:
  7.4 84.9 %copy-start = (bf16[4,256,1024]{2,1,0:T(8,128)(2,1)S(1)}, bf16[4,256,1024]{2,1,0:T(8,128)(2,1)}, u32[]{:S(2)}) copy-start(bf16[4,256,1024]{2,1,0:T(8,128)(2,1)} %param.25) | copy-start | bytes 6291460
  7.4 77.2 %all-gather.2.cloned.1.call-start = ((), (), s32[]{:S(2)}) async-start(), calls=%async_computation.5 | async-start | bytes 8257536 | tf_op jit(solution)/shard_map/all_gather | solution.py:62
  14.3 26.3 %copy-start.5 = (bf16[48,1024]{1,0:T(8,128)(2,1)S(1)}, bf16[48,1024]{1,0:T(8,128)(2,1)}, u32[]{:S(2)}) copy-start(bf16[48,1024]{1,0:T(8,128)(2,1)} %param.15) | copy-start | bytes 294916
  14.3 26.3 %copy-start.7 = (s32[3]{0:T(128)S(1)}, s32[3]{0:T(128)}, u32[]{:S(2)}) copy-start(s32[3]{0:T(128)} %param.14) | copy-start | bytes 40
  14.3 26.5 %copy-start.6 = (bf16[1024,16]{0,1:T(8,128)(2,1)S(1)}, bf16[1024,16]{0,1:T(8,128)(2,1)}, u32[]{:S(2)}) copy-start(bf16[1024,16]{0,1:T(8,128)(2,1)} %param.16) | copy-start | bytes 98308
  40.5 87.6 %all-reduce.5.cloned.1.call-start = ((), (), s32[]{:S(2)}) async-start(), calls=%async_computation.4 | async-start | bytes 262144 | tf_op jit(solution)/shard_map/pmax | solution.py:23
  47.8 121.3 %reduce-scatter.5.cloned.1.call-start = ((), (), s32[]{:S(2)}) async-start(), calls=%async_computation.6 | async-start | bytes 8257536 | tf_op jit(solution)/shard_map/reduce_scatter | solution.py:67
  101.6 117.1 %all-reduce.7.cloned.1.call-start = ((), (), s32[]{:S(2)}) async-start(), calls=%async_computation.7 | async-start | bytes 262144
  129.7 7.7 %copy-start.4 = (bf16[1024,1024]{1,0:T(8,128)(2,1)S(1)}, bf16[1024,1024]{1,0:T(8,128)(2,1)}, u32[]{:S(2)}) copy-start(bf16[1024,1024]{1,0:T(8,128)(2,1)} %param.17) | copy-start | bytes 6291460
  129.7 122.2 %reduce-scatter.7.cloned.1.call-start = ((), (), s32[]{:S(2)}) async-start(), calls=%async_computation.8 | async-start | bytes 4456448
  168.9 8.1 %copy-start.2 = (s32[128,2]{0,1:T(2,128)S(1)}, s32[128,2]{0,1:T(2,128)}, u32[]{:S(2)}) copy-start(s32[128,2]{0,1:T(2,128)} %param.21) | copy-start | bytes 3076
  168.9 8.6 %copy-start.3 = (f32[128,2]{0,1:T(2,128)S(1)}, f32[128,2]{0,1:T(2,128)}, u32[]{:S(2)}) copy-start(f32[128,2]{0,1:T(2,128)} %param.22) | copy-start | bytes 3076
  168.9 9.3 %copy-start.8 = (u32[128]{0:T(128)S(1)}, u32[128]{0:T(128)}, u32[]{:S(2)}) copy-start(u32[128]{0:T(128)} %constant.60) | copy-start | bytes 1540
  171.9 81.7 %all-to-all-start.1 = ((bf16[16,4,7,1024]{3,1,2,0:T(4,128)(2,1)}), bf16[16,4,7,1024]{3,1,2,0:T(4,128)(2,1)S(1)}, u32[]{:S(2)}, u32[]{:S(2)}) async-start(bf16[16,4,7,1024]{3,1,2,0:T(4,128)(2,1)} %copy.50), calls=%async_computation.2 | async-start | bytes 1835008 | tf_op jit(solution)/shard_map/all_to_all | solution.py:70
  255.0 8.5 %copy-start.1 = (bf16[4,256,1024]{2,1,0:T(8,128)(2,1)S(1)}, bf16[4,256,1024]{2,1,0:T(8,128)(2,1)}, u32[]{:S(2)}) copy-start(bf16[4,256,1024]{2,1,0:T(8,128)(2,1)} %param.25) | copy-start | bytes 6291460
Sparse Core Ops, SparseCore 0:
  40.6 43.9 all-gather.1
  101.8 47.5 reduce-scatter.4
  169.1 82.8 reduce-scatter.6
Sparse Core Ops, SparseCore 1:
  47.9 80.1 all-reduce.4
  131.1 87.5 all-reduce.6

commit v2 on v0

v2 whole, which is shorter than its diff:
```python
import jax
import jax.numpy as jnp
from jax import lax
from jax.experimental import pallas as pl
from jax.experimental.pallas import tpu as pltpu
from jax.sharding import PartitionSpec as P

MESH = pl.DeviceIdType.MESH
BF16 = jnp.bfloat16
F32 = jnp.float32
D = 1024
H = 16
VARS = 3
ROWS = 128
EXPERTS = 64
GROUP = 4
FF = 256
CAP = 7
NT = 16
NZ = 4
BLK = NT * CAP
HALF = NZ * BLK
PAIR = NT * 16
XSLOTS = 3


def dot(a, b):
    return jnp.dot(a, b, preferred_element_type=F32)


def dot_t(a, b):
    return lax.dot_general(a, b, (((0,), (0,)), ((), ())), preferred_element_type=F32)


def iota(shape, dim):
    return lax.broadcasted_iota(jnp.int32, shape, dim)


def kernel(
    x,
    ids,
    embed,
    svec,
    vw,
    ow,
    half,
    gain,
    routes,
    rweights,
    wg,
    wu,
    wd,
    out,
    wgu,
    wdn,
    vwb,
    owb,
    xbuf,
    lab,
    svt,
    spread,
    chi,
    clo,
    pk,
    rb,
    ag,
    pt,
    sb,
    zr1,
    zr2,
    so,
    rs,
    rr,
    ns,
    nr,
    st_s,
    st_r,
    acc,
    xsem,
    wsem,
    a_s,
    a_r,
    g_s,
    g_r,
    p_s,
    p_r,
    r_s,
    r_r,
    n_s,
    n_r,
    t_s,
    t_r,
    own_sem,
):
    me = lax.axis_index("tok")
    ex = lax.axis_index("exp")
    z = ex // 2
    core = ex % 2
    up = (me, ((z + 1) % NZ) * 2 + core)
    down = (me, ((z + NZ - 1) % NZ) * 2 + core)
    sib = (me, z * 2 + (1 - core))

    def tok_dev(o):
        return ((me + o) % NT, ex)

    def remote(src, dst, send, recv, dev):
        return pltpu.make_async_remote_copy(
            src_ref=src, dst_ref=dst, send_sem=send, recv_sem=recv, device_id=dev, device_id_type=MESH
        )

    def rows_at(start, size):
        return pl.ds(pl.multiple_of(start, 16), size)

    def x_copy(o):
        slot = o % XSLOTS
        return pltpu.make_async_copy(x.at[:, (me + o) % NT], xbuf.at[slot], xsem.at[slot])

    vw_copy = pltpu.make_async_copy(vw, vwb, wsem.at[0])
    ow_copy = pltpu.make_async_copy(ow, owb, wsem.at[1])
    w_copies = []
    for e in range(GROUP):
        w_copies.append(
            (
                pltpu.make_async_copy(wg.at[e], wgu.at[e, :, 0:FF], wsem.at[2 + 3 * e]),
                pltpu.make_async_copy(wu.at[e], wgu.at[e, :, FF : 2 * FF], wsem.at[3 + 3 * e]),
                pltpu.make_async_copy(wd.at[e], wdn.at[e], wsem.at[4 + 3 * e]),
            )
        )

    barrier = pltpu.get_barrier_semaphore()
    greeted = [tok_dev(o) for o in range(1, NT)] + [up, down, sib]
    for dev in greeted:
        pl.semaphore_signal(barrier, inc=1, device_id=dev, device_id_type=MESH)

    vw_copy.start()
    for o in range(1, 1 + XSLOTS):
        x_copy(o).start()
    for group in w_copies:
        for copy in group:
            copy.start()
    ow_copy.start()

    level = half[...].astype(F32)
    scale = lax.rsqrt(jnp.mean(level * level, axis=-1, keepdims=True) + 1e-06)
    normed = (level * scale * gain[...].astype(F32)).astype(BF16)
    route0 = routes[:, 0:1]
    route1 = routes[:, 1:2]
    experts = iota((ROWS, EXPERTS), 1)
    named0 = route0 == experts
    named1 = route1 == experts
    either = jnp.where(named0 | named1, 1.0, 0.0).astype(BF16)
    before = jnp.where(iota((ROWS, ROWS), 0) > iota((ROWS, ROWS), 1), 1.0, 0.0).astype(BF16)
    count = dot(before, either)

    def target(route, named):
        slot = jnp.sum(jnp.where(named, count, 0.0), axis=1, keepdims=True).astype(jnp.int32)
        pair = jnp.right_shift(route, 1) & 1
        return pair * PAIR + jnp.right_shift(route, 2) * 16 + (route & 1) * 8 + slot

    places = iota((ROWS, 2 * PAIR), 1)
    here0 = places == target(route0, named0)
    here1 = places == target(route1, named1)
    placing = jnp.where(here0 | here1, 1.0, 0.0).astype(BF16)
    pk[...] = dot_t(placing, normed).astype(BF16)
    weights = jnp.where(here0, rweights[:, 0:1], 0.0) + jnp.where(here1, rweights[:, 1:2], 0.0)
    high = weights.astype(BF16)
    chi[...] = high
    clo[...] = (weights - high.astype(F32)).astype(BF16)

    pl.semaphore_wait(barrier, len(greeted))

    def dispatch(p, o):
        mine = rows_at(p * PAIR + me * 16, 16)
        theirs = rows_at(p * PAIR + ((me + o) % NT) * 16, 16)
        return remote(pk.at[theirs], rb.at[mine], a_s.at[p, o], a_r.at[p, o], tok_dev(o))

    for p in range(2):
        for o in range(1, NT):
            dispatch(p, o).start()

    def dispatch_arrived(p):
        mine = rows_at(p * PAIR + me * 16, 16)
        rb[mine] = pk[mine]
        for o in range(1, NT):
            dispatch(p, o).wait_recv()

    picks = jnp.where(ids[...] == iota((VARS, embed.shape[0]), 1), 1.0, 0.0).astype(BF16)
    lab[0:VARS] = dot(picks, embed[...])
    svt[...] = jnp.transpose(svec[...].astype(F32)).astype(BF16)
    spread[...] = jnp.where(jnp.right_shift(iota((H, D), 1), 6) == iota((H, D), 0), 1.0, 0.0).astype(BF16)
    vw_copy.wait()

    def sum_copy(o):
        dest = (me + o) % NT
        return remote(ns.at[dest], nr.at[me], n_s.at[o], n_r.at[o], tok_dev(o))

    def stat_copy(o):
        dest = (me + o) % NT
        return remote(st_s.at[dest], st_r.at[me], t_s.at[o], t_r.at[o], tok_dev(o))

    def aggregate(o, _):
        dest = (me + o) % NT
        slot = o % XSLOTS
        x_copy(o).wait()
        embedded = jnp.concatenate(
            [(xbuf[slot, v].astype(F32) + lab[v : v + 1]).astype(BF16) for v in range(VARS)], axis=0
        )
        scores = lax.dot_general(
            svt[...], embedded, (((1,), (1,)), ((), ())), preferred_element_type=F32
        )
        parts = [scores[:, v * ROWS : (v + 1) * ROWS] for v in range(VARS)]
        peak = jnp.maximum(jnp.maximum(parts[0], parts[1]), parts[2])
        expo = [jnp.exp(part - peak) for part in parts]
        denom = expo[0] + expo[1] + expo[2]
        inverse = 1.0 / denom
        st_s[dest, 0:H] = peak
        st_s[dest, H : 2 * H] = denom
        values = dot(embedded, vwb[...])
        mixed = None
        for v in range(VARS):
            share = dot_t((expo[v] * inverse).astype(BF16), spread[...])
            term = share * values[v * ROWS : (v + 1) * ROWS]
            mixed = term if mixed is None else mixed + term
        ns[dest] = mixed.astype(BF16)

        @pl.when(o < NT)
        def _():
            sum_copy(o).start()
            stat_copy(o).start()

        @pl.when(o + XSLOTS <= NT)
        def _():
            x_copy(o + XSLOTS).start()

        return 0

    def aggregate_range(low, high_):
        lax.fori_loop(low, high_, aggregate, 0)

    def packed_row(col):
        return (jnp.right_shift(col, 3) & 1) * BLK + jnp.right_shift(col, 4) * CAP + (col & 7)

    mine_ag = (core * NZ + z) * BLK

    def compact(p):
        col = iota((2 * BLK, PAIR), 1)
        pick = jnp.where(
            (iota((2 * BLK, PAIR), 0) == packed_row(col)) & ((col & 7) < CAP), 1.0, 0.0
        ).astype(BF16)
        dense = dot(pick, rb[p * PAIR : (p + 1) * PAIR]).astype(BF16)
        ag[2 * p, rows_at(mine_ag, BLK)] = dense[0:BLK]
        ag[2 * p + 1, rows_at(mine_ag, BLK)] = dense[BLK : 2 * BLK]

    def low_rows(e):
        return 64 if e % 2 == 0 else 48

    def block_row(c, dz):
        return (c * NZ + (z + dz) % NZ) * BLK

    def gather_copy(e, kind):
        low = low_rows(e)
        start, size, dev = {
            0: (block_row(core, 0), BLK, up),
            1: (block_row(core, 0), BLK, down),
            2: (block_row(core, NZ - 1), low, up),
            3: (block_row(core, 1) + low, BLK - low, down),
            4: (block_row(core, 0), BLK, sib),
            5: (block_row(core, NZ - 1), BLK, sib),
            6: (block_row(core, 1), BLK, sib),
            7: (block_row(core, 2), low, sib),
            8: (block_row(core, 2) + low, BLK - low, sib),
        }[kind]
        place = ag.at[e, rows_at(start, size)]
        return remote(place, place, g_s.at[e, kind], g_r.at[e, kind], dev)

    def gather_recv(e, kind):
        low = low_rows(e)
        start, size, dev = {
            0: (block_row(core, NZ - 1), BLK, down),
            1: (block_row(core, 1), BLK, up),
            2: (block_row(core, 2), low, down),
            3: (block_row(core, 2) + low, BLK - low, up),
            4: (block_row(1 - core, 0), BLK, sib),
            5: (block_row(1 - core, NZ - 1), BLK, sib),
            6: (block_row(1 - core, 1), BLK, sib),
            7: (block_row(1 - core, 2), low, sib),
            8: (block_row(1 - core, 2) + low, BLK - low, sib),
        }[kind]
        place = ag.at[e, rows_at(start, size)]
        remote(place, place, g_s.at[e, kind], g_r.at[e, kind], dev).wait_recv()

    def gather_first(e):
        gather_copy(e, 0).start()
        gather_copy(e, 1).start()
        gather_copy(e, 4).start()

    def gather_second(e):
        gather_recv(e, 0)
        gather_copy(e, 2).start()
        gather_copy(e, 5).start()
        gather_recv(e, 1)
        gather_copy(e, 3).start()
        gather_copy(e, 6).start()

    def gather_third(e):
        gather_recv(e, 2)
        gather_copy(e, 7).start()
        gather_recv(e, 3)
        gather_copy(e, 8).start()

    def ffn(e, start):
        rows = rows_at(start, HALF)
        both = dot(ag[e, rows], wgu[e])
        gate = both[:, 0:FF]
        hidden = (gate / (1.0 + jnp.exp(-gate)) * both[:, FF : 2 * FF]).astype(BF16)
        pt[e, rows] = dot(hidden, wdn[e]).astype(BF16)

    def sibling_copy(e):
        return remote(
            pt.at[e, rows_at((1 - core) * HALF, HALF)], sb.at[e], p_s.at[e, 0], p_r.at[e, 0], sib
        )

    def experts_of(e):
        for copy in w_copies[e]:
            copy.wait()
        ffn(e, core * HALF)
        for kind in range(4, 9):
            gather_recv(e, kind)
        ffn(e, (1 - core) * HALF)
        sibling_copy(e).start()

    def part(e, dz, start, size):
        return pt.at[e, rows_at(block_row(core, dz) + start, size)]

    def sum_step(e, kind):
        low = low_rows(e)
        src, dst, dev = {
            1: (part(e, 2, 0, low), zr1.at[e, 0, 0:low], up),
            2: (part(e, 2, low, BLK - low), zr1.at[e, 1, 0 : BLK - low], down),
            3: (part(e, 1, low, BLK - low), zr2.at[e, 0, low:BLK], up),
            4: (part(e, 1, 0, low), zr2.at[e, 0, 0:low], up),
            5: (part(e, NZ - 1, 0, low), zr2.at[e, 1, 0:low], down),
            6: (part(e, NZ - 1, low, BLK - low), zr2.at[e, 1, low:BLK], down),
        }[kind]
        return remote(src, dst, p_s.at[e, kind], p_r.at[e, kind], dev)

    def add_sibling(e, dz):
        here = rows_at(block_row(core, dz), BLK)
        there = rows_at(((z + dz) % NZ) * BLK, BLK)
        pt[e, here] = (pt[e, here].astype(F32) + sb[e, there].astype(F32)).astype(BF16)

    def sum_first(e):
        sibling_copy(e).wait_recv()
        add_sibling(e, 2)
        sum_step(e, 1).start()
        sum_step(e, 2).start()
        add_sibling(e, 1)
        sum_step(e, 3).start()
        add_sibling(e, NZ - 1)
        sum_step(e, 5).start()
        add_sibling(e, 0)

    def sum_second(e):
        low = low_rows(e)
        sum_step(e, 1).wait_recv()
        here = rows_at(block_row(core, 1), low)
        pt[e, here] = (pt[e, here].astype(F32) + zr1[e, 0, 0:low].astype(F32)).astype(BF16)
        sum_step(e, 4).start()
        sum_step(e, 2).wait_recv()
        here = rows_at(block_row(core, NZ - 1) + low, BLK - low)
        pt[e, here] = (pt[e, here].astype(F32) + zr1[e, 1, 0 : BLK - low].astype(F32)).astype(BF16)
        sum_step(e, 6).start()

    def sum_third(e):
        for kind in range(3, 7):
            sum_step(e, kind).wait_recv()
        here = rows_at(block_row(core, 0), BLK)
        total = pt[e, here].astype(F32) + zr2[e, 0].astype(F32) + zr2[e, 1].astype(F32)
        start = (e % 2) * BLK
        so[e // 2, start : start + BLK] = total.astype(BF16)

    def give_back(p, o):
        mine = rows_at(p * PAIR + me * 16, 16)
        theirs = rows_at(p * PAIR + ((me + o) % NT) * 16, 16)
        return remote(rs.at[theirs], rr.at[mine], r_s.at[p, o], r_r.at[p, o], tok_dev(o))

    def send_back(p):
        row = iota((PAIR, 2 * BLK), 0)
        place = jnp.where(
            (iota((PAIR, 2 * BLK), 1) == packed_row(row)) & ((row & 7) < CAP), 1.0, 0.0
        ).astype(BF16)
        rs[p * PAIR : (p + 1) * PAIR] = dot(place, so[p]).astype(BF16)
        for o in range(1, NT):
            give_back(p, o).start()
        mine = rows_at(p * PAIR + me * 16, 16)
        rr[mine] = rs[mine]

    def merge():
        for o in range(1, NT):
            stat_copy(o).wait_recv()
            sum_copy(o).wait_recv()
        peak = st_r[0, 0:H]
        for j in range(1, NT):
            peak = jnp.maximum(peak, st_r[j, 0:H])
        total = jnp.zeros((H, ROWS), F32)
        for j in range(NT):
            total = total + st_r[j, H : 2 * H] * jnp.exp(st_r[j, 0:H] - peak)
        inverse = 1.0 / total
        acc[...] = jnp.zeros_like(acc)

        def add(j, _):
            share = st_r[j, H : 2 * H] * jnp.exp(st_r[j, 0:H] - peak) * inverse
            acc[...] += dot_t(share.astype(BF16), spread[...]) * nr[j].astype(F32)
            return 0

        lax.fori_loop(0, NT, add, 0)
        ow_copy.wait()
        acc[...] = dot(acc[...].astype(BF16), owb[...])

    def take_back(p):
        for o in range(1, NT):
            give_back(p, o).wait_recv()
        back = rr[p * PAIR : (p + 1) * PAIR]
        cols = pl.ds(p * PAIR, PAIR)
        acc[...] += dot(chi[:, cols], back) + dot(clo[:, cols], back)

    aggregate_range(1, 6)
    dispatch_arrived(0)
    compact(0)
    gather_first(0)
    gather_first(1)
    aggregate_range(6, 9)
    dispatch_arrived(1)
    compact(1)
    gather_second(0)
    gather_first(2)
    aggregate_range(9, 12)
    gather_second(1)
    gather_first(3)
    gather_third(0)
    experts_of(0)
    aggregate_range(12, 14)
    gather_second(2)
    sum_first(0)
    gather_third(1)
    experts_of(1)
    aggregate_range(14, 17)
    own_sum = pltpu.make_async_copy(ns.at[me], nr.at[me], own_sem.at[0])
    own_stat = pltpu.make_async_copy(st_s.at[me], st_r.at[me], own_sem.at[1])
    own_sum.start()
    own_stat.start()
    gather_second(3)
    sum_second(0)
    sum_first(1)
    gather_third(2)
    experts_of(2)
    sum_third(0)
    sum_second(1)
    sum_first(2)
    gather_third(3)
    experts_of(3)
    sum_third(1)
    send_back(0)
    sum_second(2)
    sum_first(3)
    own_sum.wait()
    own_stat.wait()
    merge()
    sum_second(3)
    sum_third(2)
    take_back(0)
    sum_third(3)
    send_back(1)
    take_back(1)
    out[...] = acc[...].astype(BF16)

    for p in range(2):
        for o in range(1, NT):
            dispatch(p, o).wait_send()
            give_back(p, o).wait_send()
    for o in range(1, NT):
        sum_copy(o).wait_send()
        stat_copy(o).wait_send()
    for e in range(GROUP):
        for kind in range(9):
            gather_copy(e, kind).wait_send()
        sibling_copy(e).wait_send()
        for kind in range(1, 7):
            sum_step(e, kind).wait_send()


def shards(
    x_var,
    var_ids,
    var_embed,
    score_vecs,
    v_weight,
    out_weight,
    second_half,
    norm_gain,
    routes,
    route_weights,
    w_gate,
    w_up,
    w_down,
):
    vmem = pl.BlockSpec(memory_space=pltpu.VMEM)
    anywhere = pl.BlockSpec(memory_space=pl.ANY)
    dma = pltpu.SemaphoreType.DMA
    return pl.pallas_call(
        kernel,
        out_shape=jax.ShapeDtypeStruct((ROWS, D), BF16),
        in_specs=[
            anywhere,
            vmem,
            vmem,
            vmem,
            anywhere,
            anywhere,
            vmem,
            vmem,
            vmem,
            vmem,
            anywhere,
            anywhere,
            anywhere,
        ],
        out_specs=vmem,
        scratch_shapes=[
            pltpu.VMEM((GROUP, D, 2 * FF), BF16),
            pltpu.VMEM((GROUP, FF, D), BF16),
            pltpu.VMEM((D, D), BF16),
            pltpu.VMEM((D, D), BF16),
            pltpu.VMEM((XSLOTS, VARS, ROWS, D), BF16),
            pltpu.VMEM((8, D), F32),
            pltpu.VMEM((H, D), BF16),
            pltpu.VMEM((H, D), BF16),
            pltpu.VMEM((ROWS, 2 * PAIR), BF16),
            pltpu.VMEM((ROWS, 2 * PAIR), BF16),
            pltpu.VMEM((2 * PAIR, D), BF16),
            pltpu.VMEM((2 * PAIR, D), BF16),
            pltpu.VMEM((GROUP, 2 * HALF, D), BF16),
            pltpu.VMEM((GROUP, 2 * HALF, D), BF16),
            pltpu.VMEM((GROUP, HALF, D), BF16),
            pltpu.VMEM((GROUP, 2, 64, D), BF16),
            pltpu.VMEM((GROUP, 2, BLK, D), BF16),
            pltpu.VMEM((2, 2 * BLK, D), BF16),
            pltpu.VMEM((2 * PAIR, D), BF16),
            pltpu.VMEM((2 * PAIR, D), BF16),
            pltpu.VMEM((NT, ROWS, D), BF16),
            pltpu.VMEM((NT, ROWS, D), BF16),
            pltpu.VMEM((NT, 2 * H, ROWS), F32),
            pltpu.VMEM((NT, 2 * H, ROWS), F32),
            pltpu.VMEM((ROWS, D), F32),
            dma((XSLOTS,)),
            dma((2 + 3 * GROUP,)),
            dma((2, NT)),
            dma((2, NT)),
            dma((GROUP, 9)),
            dma((GROUP, 9)),
            dma((GROUP, 7)),
            dma((GROUP, 7)),
            dma((2, NT)),
            dma((2, NT)),
            dma((NT,)),
            dma((NT,)),
            dma((NT,)),
            dma((NT,)),
            dma((2,)),
        ],
        compiler_params=pltpu.CompilerParams(
            collective_id=0, has_side_effects=True, vmem_limit_bytes=62 * 2**20
        ),
        cost_estimate=pl.CostEstimate(
            flops=20_000_000_000, bytes_accessed=24_000_000, transcendentals=1_000_000
        ),
    )(
        x_var,
        var_ids.reshape(VARS, 1),
        var_embed,
        score_vecs,
        v_weight,
        out_weight,
        second_half,
        norm_gain.reshape(1, D),
        routes,
        route_weights,
        w_gate,
        w_up,
        w_down,
    )


def solution(mesh):
    in_specs = (
        P("tok", None, "exp", None),
        P("tok"),
        P(),
        P(),
        P(),
        P(),
        P(("tok", "exp"), None),
        P(),
        P(("tok", "exp"), None),
        P(("tok", "exp"), None),
        P("tok", None, "exp"),
        P("tok", None, "exp"),
        P("tok", "exp", None),
    )
    out_specs = P(("tok", "exp"), None)
    return jax.shard_map(shards, mesh=mesh, in_specs=in_specs, out_specs=out_specs, check_vma=False)
```

time: 370 us -> 124 us (0.34)
  the two profiles are of different devices: /device:TPU:0 before, /device:TPU:36 now
where the time goes in v2:
time: 124 us
  Pallas kernels  115 us (93%)
  local copies, waits for them, and re-layouts  8.64 us (7%)
    pallas_call x1, Pallas kernels, shards(): pl.pallas_call(kernel, out_shape=jax.ShapeDtypeStruct((ROWS, D), BF16), i...  115 us
    unnamed x4, local copies, waits for them, and re-layouts  6.08 us

profile of v2, /device:TPU:36, one launch (start us, length us, event | category | flops | bytes accessed | tf_op | source)
XLA Modules:
  0.0 123.9 jit_solution(8743848966000765969)
XLA Ops:
  0.0 1.3 %copy.14.ids = s32[3,1]{1,0:T(4,128)} copy(s32[3,1]{0,1:T(1,128)} %bitcast.1) | data formatting | bytes 24 | tf_op jit(solution)/shard_map/reshape | solution.py:579
  1.3 1.3 %reshape.7.gain = bf16[1,1024]{1,0:T(2,128)(2,1)} reshape(bf16[1024]{0:T(1024)(128)(2,1)} %param.20) | data formatting | bytes 4096 | tf_op jit(solution)/shard_map/reshape | solution.py:585
  2.6 1.4 %copy.16.routes = s32[128,2]{1,0:T(8,128)} copy(s32[128,2]{0,1:T(2,128)} %param.21) | data formatting | bytes 2048 | tf_op args[8]
  4.0 1.4 %copy.17.rweights = f32[128,2]{1,0:T(8,128)} copy(f32[128,2]{0,1:T(2,128)} %param.22) | data formatting | bytes 2048 | tf_op args[9]
  5.4 1.6 %copy.15.svec = bf16[1024,16]{1,0:T(8,128)(2,1)} copy(bf16[1024,16]{0,1:T(8,128)(2,1)} %param.16) | data formatting | bytes 65536 | tf_op args[3]
  7.0 115.2 %shard_map.127 = bf16[128,1024]{1,0:T(8,128)(2,1)} custom-call(bf16[3,16,128,1024]{3,2,1,0:T(8,128)(2,1)} %x.1, s32[3,1]{1,0:T(4,128)} %copy.14.ids, bf16[48,1024]{1,0:T(8,128)(2,1)} %embed.1, bf16[1024,16]{1,0:T(8,128)(2,1)} %copy.15.svec, bf16[1024,1024]{1,0:T(8,128)(2,1)} %vw.1, bf16[1024,1024]{1,0:T(8,128)(2,1)} %ow.1, bf16[128,1024]{1,0:T(8,128)(2,1)} %half.1, ...), custom_call_target="tpu_custom_call" | custom-call | flops 20000000000 | bytes 24000000 | tf_op jit(solution)/shard_map/pallas_call | solution.py:510
  122.2 1.7 %copy.19 = bf16[128,1024]{1,0:T(8,128)(2,1)} copy(bf16[128,1024]{1,0:T(8,128)(2,1)} %shard_map.127) | data formatting | bytes 524288

commit v3 on v2

--- a/solution.py
+++ b/solution.py
@@ -20,7 +20,9 @@
 NZ = 4
 BLK = NT * CAP
 HALF = NZ * BLK
-PAIR = NT * 16
+WIDE = D // 2
+HH = H // 2
+MSG = NT * 16
 XSLOTS = 3
 
 
@@ -56,11 +58,11 @@
     vwb,
     owb,
     xbuf,
+    hbuf,
     lab,
-    svt,
+    svp,
     spread,
-    chi,
-    clo,
+    comb,
     pk,
     rb,
     ag,
@@ -72,9 +74,13 @@
     rs,
     rr,
     ns,
-    nr,
+    n1r,
+    n2s,
+    n2r,
     st_s,
-    st_r,
+    st1r,
+    st2s,
+    st2r,
     acc,
     xsem,
     wsem,
@@ -86,16 +92,21 @@
     p_r,
     r_s,
     r_r,
-    n_s,
-    n_r,
-    t_s,
-    t_r,
-    own_sem,
+    n1_s,
+    n1_r,
+    t1_s,
+    t1_r,
+    n2_s,
+    n2_r,
+    t2_s,
+    t2_r,
 ):
     me = lax.axis_index("tok")
     ex = lax.axis_index("exp")
     z = ex // 2
     core = ex % 2
+    y = me // 4
+    xx = me % 4
     up = (me, ((z + 1) % NZ) * 2 + core)
     down = (me, ((z + NZ - 1) % NZ) * 2 + core)
     sib = (me, z * 2 + (1 - core))
@@ -111,9 +122,20 @@
     def rows_at(start, size):
         return pl.ds(pl.multiple_of(start, 16), size)
 
+    def along_x(dx):
+        return (y * 4 + (xx + dx) % 4, ex)
+
+    def along_y(dy):
+        return (((y + dy) % 4) * 4 + xx, ex)
+
+    def offsets(o):
+        return (o + 1 + o // 4) % 4, (o + 1) % 4
+
     def x_copy(o):
         slot = o % XSLOTS
-        return pltpu.make_async_copy(x.at[:, (me + o) % NT], xbuf.at[slot], xsem.at[slot])
+        dy, dx = offsets(o)
+        dest = ((y + dy) % 4) * 4 + (xx + dx) % 4
+        return pltpu.make_async_copy(x.at[:, dest], xbuf.at[slot], xsem.at[slot])
 
     vw_copy = pltpu.make_async_copy(vw, vwb, wsem.at[0])
     ow_copy = pltpu.make_async_copy(ow, owb, wsem.at[1])
@@ -127,108 +149,145 @@
             )
         )
 
+    half_copy = pltpu.make_async_copy(half, hbuf, wsem.at[2 + 3 * GROUP])
+    half_copy.start()
     barrier = pltpu.get_barrier_semaphore()
     greeted = [tok_dev(o) for o in range(1, NT)] + [up, down, sib]
     for dev in greeted:
         pl.semaphore_signal(barrier, inc=1, device_id=dev, device_id_type=MESH)
 
     vw_copy.start()
-    for o in range(1, 1 + XSLOTS):
+    for o in range(XSLOTS):
         x_copy(o).start()
     for group in w_copies:
         for copy in group:
             copy.start()
     ow_copy.start()
 
-    level = half[...].astype(F32)
-    scale = lax.rsqrt(jnp.mean(level * level, axis=-1, keepdims=True) + 1e-06)
-    normed = (level * scale * gain[...].astype(F32)).astype(BF16)
-    route0 = routes[:, 0:1]
-    route1 = routes[:, 1:2]
-    experts = iota((ROWS, EXPERTS), 1)
+    route0 = routes[0:1, :]
+    route1 = routes[1:2, :]
+    experts = iota((EXPERTS, ROWS), 0)
     named0 = route0 == experts
     named1 = route1 == experts
     either = jnp.where(named0 | named1, 1.0, 0.0).astype(BF16)
-    before = jnp.where(iota((ROWS, ROWS), 0) > iota((ROWS, ROWS), 1), 1.0, 0.0).astype(BF16)
-    count = dot(before, either)
+    before = jnp.where(iota((ROWS, ROWS), 0) < iota((ROWS, ROWS), 1), 1.0, 0.0).astype(BF16)
+    count = dot(either, before)
 
     def target(route, named):
-        slot = jnp.sum(jnp.where(named, count, 0.0), axis=1, keepdims=True).astype(jnp.int32)
-        pair = jnp.right_shift(route, 1) & 1
-        return pair * PAIR + jnp.right_shift(route, 2) * 16 + (route & 1) * 8 + slot
-
-    places = iota((ROWS, 2 * PAIR), 1)
-    here0 = places == target(route0, named0)
-    here1 = places == target(route1, named1)
-    placing = jnp.where(here0 | here1, 1.0, 0.0).astype(BF16)
-    pk[...] = dot_t(placing, normed).astype(BF16)
-    weights = jnp.where(here0, rweights[:, 0:1], 0.0) + jnp.where(here1, rweights[:, 1:2], 0.0)
-    high = weights.astype(BF16)
-    chi[...] = high
-    clo[...] = (weights - high.astype(F32)).astype(BF16)
+        slot = jnp.sum(jnp.where(named, count, 0.0), axis=0, keepdims=True).astype(jnp.int32)
+        return route * 8 + slot
+
+    target0 = target(route0, named0)
+    target1 = target(route1, named1)
+    half_copy.wait()
+    level = hbuf[...].astype(F32)
+    scale = lax.rsqrt(jnp.mean(level * level, axis=-1, keepdims=True) + 1e-06)
+    normed = (level * scale * gain[...].astype(F32).reshape(1, D)).astype(BF16)
+    msg_row = iota((MSG, ROWS), 0)
+    msg_key = jnp.right_shift(msg_row, 4) * (GROUP * 8) + (msg_row & 7)
+    second = (jnp.right_shift(iota((MSG, WIDE), 0), 3) & 1) == 1
+
+    def halves(full):
+        return jnp.where(second, full[:, WIDE:], full[:, :WIDE]).astype(BF16)
+
+    def here(e):
+        return msg_key == target0 - e * 8, msg_key == target1 - e * 8
+
+    for e in range(GROUP):
+        here0, here1 = here(e)
+        placing = jnp.where(here0 | here1, 1.0, 0.0).astype(BF16)
+        pk[e] = halves(dot(placing, normed))
 
     pl.semaphore_wait(barrier, len(greeted))
 
-    def dispatch(p, o):
-        mine = rows_at(p * PAIR + me * 16, 16)
-        theirs = rows_at(p * PAIR + ((me + o) % NT) * 16, 16)
-        return remote(pk.at[theirs], rb.at[mine], a_s.at[p, o], a_r.at[p, o], tok_dev(o))
-
-    for p in range(2):
+    def msg(i):
+        return rows_at(i * 16, 16)
+
+    def dispatch(e, o):
+        there = (me + o) % NT
+        return remote(pk.at[e, msg(there)], rb.at[e, msg(me)], a_s.at[e, o], a_r.at[e, o], tok_dev(o))
+
+    for e in range(GROUP):
         for o in range(1, NT):
-            dispatch(p, o).start()
-
-    def dispatch_arrived(p):
-        mine = rows_at(p * PAIR + me * 16, 16)
-        rb[mine] = pk[mine]
+            dispatch(e, o).start()
+
+    def dispatch_arrived(e):
+        rb[e, msg(me)] = pk[e, msg(me)]
         for o in range(1, NT):
-            dispatch(p, o).wait_recv()
-
-    picks = jnp.where(ids[...] == iota((VARS, embed.shape[0]), 1), 1.0, 0.0).astype(BF16)
-    lab[0:VARS] = dot(picks, embed[...])
-    svt[...] = jnp.transpose(svec[...].astype(F32)).astype(BF16)
+            dispatch(e, o).wait_recv()
+
+    msg_half = jnp.right_shift(msg_row, 3) & 1
+    for e in range(GROUP):
+        here0, here1 = here(e)
+        weights = jnp.where(here0, rweights[0:1, :], 0.0) + jnp.where(here1, rweights[1:2, :], 0.0)
+        for side in range(2):
+            turned = jnp.transpose(jnp.where(msg_half == side, weights, 0.0))
+            high = turned.astype(BF16)
+            comb[e, side, 0:ROWS] = high
+            comb[e, side, ROWS : 2 * ROWS] = (turned - high.astype(F32)).astype(BF16)
+
+    picks = jnp.where(ids[...] == iota((embed.shape[0], VARS), 0), 1.0, 0.0).astype(BF16)
+    lab[0:VARS] = dot_t(picks, embed[...])
+    turned_scores = jnp.concatenate([svec[...].astype(F32), jnp.zeros((128 - H, D), F32)], axis=0)
+    svp[...] = jnp.transpose(turned_scores).astype(BF16)
     spread[...] = jnp.where(jnp.right_shift(iota((H, D), 1), 6) == iota((H, D), 0), 1.0, 0.0).astype(BF16)
     vw_copy.wait()
 
-    def sum_copy(o):
-        dest = (me + o) % NT
-        return remote(ns.at[dest], nr.at[me], n_s.at[o], n_r.at[o], tok_dev(o))
-
-    def stat_copy(o):
-        dest = (me + o) % NT
-        return remote(st_s.at[dest], st_r.at[me], t_s.at[o], t_r.at[o], tok_dev(o))
+    def sum_one(side, dy, dx):
+        k = dy * 4 + dx
+        if side == 0:
+            slot, dev = (dx - 1) * 4 + dy, along_x(dx)
+        else:
+            slot, dev = (dy - 1) * 4 + dx, along_y(dy)
+        return (
+            remote(ns.at[k, side], n1r.at[side, slot], n1_s.at[side, k], n1_r.at[side, k], dev),
+            remote(st_s.at[k, side], st1r.at[side, slot], t1_s.at[side, k], t1_r.at[side, k], dev),
+        )
+
+    def sum_two(side, d):
+        dev = along_y(d) if side == 0 else along_x(d)
+        return (
+            remote(n2s.at[side, d], n2r.at[side, d - 1], n2_s.at[side, d], n2_r.at[side, d], dev),
+            remote(st2s.at[side, d], st2r.at[side, d - 1], t2_s.at[side, d], t2_r.at[side, d], dev),
+        )
 
     def aggregate(o, _):
-        dest = (me + o) % NT
+        dy, dx = offsets(o)
+        k = dy * 4 + dx
         slot = o % XSLOTS
         x_copy(o).wait()
         embedded = jnp.concatenate(
             [(xbuf[slot, v].astype(F32) + lab[v : v + 1]).astype(BF16) for v in range(VARS)], axis=0
         )
-        scores = lax.dot_general(
-            svt[...], embedded, (((1,), (1,)), ((), ())), preferred_element_type=F32
-        )
-        parts = [scores[:, v * ROWS : (v + 1) * ROWS] for v in range(VARS)]
+        scores = dot(embedded, svp[...])
+        parts = [jnp.transpose(scores[v * ROWS : (v + 1) * ROWS])[0:H] for v in range(VARS)]
         peak = jnp.maximum(jnp.maximum(parts[0], parts[1]), parts[2])
         expo = [jnp.exp(part - peak) for part in parts]
         denom = expo[0] + expo[1] + expo[2]
         inverse = 1.0 / denom
-        st_s[dest, 0:H] = peak
-        st_s[dest, H : 2 * H] = denom
+        for side in range(2):
+            st_s[k, side, 0:HH] = peak[side * HH : (side + 1) * HH]
+            st_s[k, side, HH : 2 * HH] = denom[side * HH : (side + 1) * HH]
         values = dot(embedded, vwb[...])
         mixed = None
         for v in range(VARS):
             share = dot_t((expo[v] * inverse).astype(BF16), spread[...])
             term = share * values[v * ROWS : (v + 1) * ROWS]
             mixed = term if mixed is None else mixed + term
-        ns[dest] = mixed.astype(BF16)
-
-        @pl.when(o < NT)
+        ns[k, 0] = mixed[:, :WIDE].astype(BF16)
+        ns[k, 1] = mixed[:, WIDE:].astype(BF16)
+
+        @pl.when(dx > 0)
         def _():
-            sum_copy(o).start()
-            stat_copy(o).start()
-
-        @pl.when(o + XSLOTS <= NT)
+            for copy in sum_one(0, dy, dx):
+                copy.start()
+
+        @pl.when(dy > 0)
+        def _():
+            for copy in sum_one(1, dy, dx):
+                copy.start()
+
+        @pl.when(o + XSLOTS < NT)
         def _():
             x_copy(o + XSLOTS).start()
 
@@ -237,19 +296,17 @@
     def aggregate_range(low, high_):
         lax.fori_loop(low, high_, aggregate, 0)
 
-    def packed_row(col):
-        return (jnp.right_shift(col, 3) & 1) * BLK + jnp.right_shift(col, 4) * CAP + (col & 7)
-
     mine_ag = (core * NZ + z) * BLK
 
-    def compact(p):
-        col = iota((2 * BLK, PAIR), 1)
-        pick = jnp.where(
-            (iota((2 * BLK, PAIR), 0) == packed_row(col)) & ((col & 7) < CAP), 1.0, 0.0
-        ).astype(BF16)
-        dense = dot(pick, rb[p * PAIR : (p + 1) * PAIR]).astype(BF16)
-        ag[2 * p, rows_at(mine_ag, BLK)] = dense[0:BLK]
-        ag[2 * p + 1, rows_at(mine_ag, BLK)] = dense[BLK : 2 * BLK]
+    def packed_row(row):
+        return jnp.where((row & 7) < CAP, jnp.right_shift(row, 4) * CAP + (row & 7), -1)
+
+    def compact(e):
+        col = iota((BLK, MSG), 1)
+        match = iota((BLK, MSG), 0) == packed_row(col)
+        for side in range(2):
+            pick = jnp.where(match & ((jnp.right_shift(col, 3) & 1) == side), 1.0, 0.0).astype(BF16)
+            ag[e, rows_at(mine_ag, BLK), side * WIDE : (side + 1) * WIDE] = dot(pick, rb[e]).astype(BF16)
 
     def low_rows(e):
         return 64 if e % 2 == 0 else 48
@@ -376,117 +433,145 @@
             sum_step(e, kind).wait_recv()
         here = rows_at(block_row(core, 0), BLK)
         total = pt[e, here].astype(F32) + zr2[e, 0].astype(F32) + zr2[e, 1].astype(F32)
-        start = (e % 2) * BLK
-        so[e // 2, start : start + BLK] = total.astype(BF16)
-
-    def give_back(p, o):
-        mine = rows_at(p * PAIR + me * 16, 16)
-        theirs = rows_at(p * PAIR + ((me + o) % NT) * 16, 16)
-        return remote(rs.at[theirs], rr.at[mine], r_s.at[p, o], r_r.at[p, o], tok_dev(o))
-
-    def send_back(p):
-        row = iota((PAIR, 2 * BLK), 0)
+        so[...] = total.astype(BF16)
+        send_back(e)
+
+    def give_back(e, o):
+        there = (me + o) % NT
+        return remote(rs.at[e, msg(there)], rr.at[e, msg(me)], r_s.at[e, o], r_r.at[e, o], tok_dev(o))
+
+    def send_back(e):
         place = jnp.where(
-            (iota((PAIR, 2 * BLK), 1) == packed_row(row)) & ((row & 7) < CAP), 1.0, 0.0
+            iota((MSG, BLK), 1) == packed_row(iota((MSG, BLK), 0)), 1.0, 0.0
         ).astype(BF16)
-        rs[p * PAIR : (p + 1) * PAIR] = dot(place, so[p]).astype(BF16)
+        rs[e] = halves(dot(place, so[...]))
         for o in range(1, NT):
-            give_back(p, o).start()
-        mine = rows_at(p * PAIR + me * 16, 16)
-        rr[mine] = rs[mine]
-
-    def merge():
-        for o in range(1, NT):
-            stat_copy(o).wait_recv()
-            sum_copy(o).wait_recv()
-        peak = st_r[0, 0:H]
-        for j in range(1, NT):
-            peak = jnp.maximum(peak, st_r[j, 0:H])
-        total = jnp.zeros((H, ROWS), F32)
-        for j in range(NT):
-            total = total + st_r[j, H : 2 * H] * jnp.exp(st_r[j, 0:H] - peak)
+            give_back(e, o).start()
+        rr[e, msg(me)] = rs[e, msg(me)]
+
+    def merged(stats, sums):
+        peak = stats[0][0:HH]
+        for stat in stats[1:]:
+            peak = jnp.maximum(peak, stat[0:HH])
+        shares = [stat[HH : 2 * HH] * jnp.exp(stat[0:HH] - peak) for stat in stats]
+        total = shares[0] + shares[1] + shares[2] + shares[3]
         inverse = 1.0 / total
-        acc[...] = jnp.zeros_like(acc)
-
-        def add(j, _):
-            share = st_r[j, H : 2 * H] * jnp.exp(st_r[j, 0:H] - peak) * inverse
-            acc[...] += dot_t(share.astype(BF16), spread[...]) * nr[j].astype(F32)
-            return 0
-
-        lax.fori_loop(0, NT, add, 0)
+        value = None
+        for share, term in zip(shares, sums):
+            wide = dot_t((share * inverse).astype(BF16), spread[0:HH, 0:WIDE])
+            piece = wide * term.astype(F32)
+            value = piece if value is None else value + piece
+        return peak, total, value
+
+    def merge_one(side, d):
+        stats, sums = [], []
+        k = d * 4 if side == 0 else d
+        stats.append(st_s[k, side])
+        sums.append(ns[k, side])
+        for first in range(1, 4):
+            dy, dx = (d, first) if side == 0 else (first, d)
+            for copy in sum_one(side, dy, dx):
+                copy.wait_recv()
+            stats.append(st1r[side, (first - 1) * 4 + d])
+            sums.append(n1r[side, (first - 1) * 4 + d])
+        peak, total, value = merged(stats, sums)
+        st2s[side, d, 0:HH] = peak
+        st2s[side, d, HH : 2 * HH] = total
+        n2s[side, d] = value.astype(BF16)
+        if d > 0:
+            for copy in sum_two(side, d):
+                copy.start()
+
+    def merge_two():
+        for side in range(2):
+            stats, sums = [st2s[side, 0]], [n2s[side, 0]]
+            for d in range(1, 4):
+                for copy in sum_two(side, d):
+                    copy.wait_recv()
+                stats.append(st2r[side, d - 1])
+                sums.append(n2r[side, d - 1])
+            acc[:, side * WIDE : (side + 1) * WIDE] = merged(stats, sums)[2]
         ow_copy.wait()
         acc[...] = dot(acc[...].astype(BF16), owb[...])
 
-    def take_back(p):
+    def take_back(e):
         for o in range(1, NT):
-            give_back(p, o).wait_recv()
-        back = rr[p * PAIR : (p + 1) * PAIR]
-        cols = pl.ds(p * PAIR, PAIR)
-        acc[...] += dot(chi[:, cols], back) + dot(clo[:, cols], back)
-
-    aggregate_range(1, 6)
+            give_back(e, o).wait_recv()
+        for side in range(2):
+            both = dot(comb[e, side], rr[e])
+            acc[:, side * WIDE : (side + 1) * WIDE] += both[0:ROWS] + both[ROWS : 2 * ROWS]
+
+    aggregate_range(0, 3)
     dispatch_arrived(0)
     compact(0)
     gather_first(0)
-    gather_first(1)
-    aggregate_range(6, 9)
     dispatch_arrived(1)
     compact(1)
+    gather_first(1)
+    aggregate_range(3, 6)
+    dispatch_arrived(2)
+    compact(2)
     gather_second(0)
     gather_first(2)
-    aggregate_range(9, 12)
+    aggregate_range(6, 9)
+    dispatch_arrived(3)
+    compact(3)
     gather_second(1)
     gather_first(3)
     gather_third(0)
+    aggregate_range(9, 10)
     experts_of(0)
-    aggregate_range(12, 14)
+    aggregate_range(10, 12)
     gather_second(2)
     sum_first(0)
     gather_third(1)
     experts_of(1)
-    aggregate_range(14, 17)
-    own_sum = pltpu.make_async_copy(ns.at[me], nr.at[me], own_sem.at[0])
-    own_stat = pltpu.make_async_copy(st_s.at[me], st_r.at[me], own_sem.at[1])
-    own_sum.start()
-    own_stat.start()
+    aggregate_range(12, 14)
     gather_second(3)
     sum_second(0)
     sum_first(1)
     gather_third(2)
     experts_of(2)
+    aggregate_range(14, 16)
     sum_third(0)
     sum_second(1)
     sum_first(2)
     gather_third(3)
     experts_of(3)
+    for d in range(1, 4):
+        merge_one(0, d)
+        merge_one(1, d)
     sum_third(1)
-    send_back(0)
     sum_second(2)
     sum_first(3)
-    own_sum.wait()
-    own_stat.wait()
-    merge()
+    merge_one(0, 0)
+    merge_one(1, 0)
+    sum_third(2)
     sum_second(3)
-    sum_third(2)
+    merge_two()
     take_back(0)
+    take_back(1)
     sum_third(3)
-    send_back(1)
-    take_back(1)
+    take_back(2)
+    take_back(3)
     out[...] = acc[...].astype(BF16)
 
-    for p in range(2):
+    for e in range(GROUP):
         for o in range(1, NT):
-            dispatch(p, o).wait_send()
-            give_back(p, o).wait_send()
-    for o in range(1, NT):
-        sum_copy(o).wait_send()
-        stat_copy(o).wait_send()
-    for e in range(GROUP):
+            dispatch(e, o).wait_send()
+            give_back(e, o).wait_send()
         for kind in range(9):
             gather_copy(e, kind).wait_send()
         sibling_copy(e).wait_send()
         for kind in range(1, 7):
             sum_step(e, kind).wait_send()
+    for d in range(4):
+        for first in range(1, 4):
+            for copy in sum_one(0, d, first) + sum_one(1, first, d):
+                copy.wait_send()
+        if d > 0:
+            for copy in sum_two(0, d) + sum_two(1, d):
+                copy.wait_send()
 
 
 def shards(
@@ -517,7 +602,7 @@
             vmem,
             anywhere,
             anywhere,
-            vmem,
+            anywhere,
             vmem,
             vmem,
             vmem,
@@ -532,41 +617,48 @@
             pltpu.VMEM((D, D), BF16),
             pltpu.VMEM((D, D), BF16),
             pltpu.VMEM((XSLOTS, VARS, ROWS, D), BF16),
+            pltpu.VMEM((ROWS, D), BF16),
             pltpu.VMEM((8, D), F32),
+            pltpu.VMEM((D, 128), BF16),
             pltpu.VMEM((H, D), BF16),
-            pltpu.VMEM((H, D), BF16),
-            pltpu.VMEM((ROWS, 2 * PAIR), BF16),
-            pltpu.VMEM((ROWS, 2 * PAIR), BF16),
-            pltpu.VMEM((2 * PAIR, D), BF16),
-            pltpu.VMEM((2 * PAIR, D), BF16),
+            pltpu.VMEM((GROUP, 2, 2 * ROWS, MSG), BF16),
+            pltpu.VMEM((GROUP, MSG, WIDE), BF16),
+            pltpu.VMEM((GROUP, MSG, WIDE), BF16),
             pltpu.VMEM((GROUP, 2 * HALF, D), BF16),
             pltpu.VMEM((GROUP, 2 * HALF, D), BF16),
             pltpu.VMEM((GROUP, HALF, D), BF16),
             pltpu.VMEM((GROUP, 2, 64, D), BF16),
             pltpu.VMEM((GROUP, 2, BLK, D), BF16),
-            pltpu.VMEM((2, 2 * BLK, D), BF16),
-            pltpu.VMEM((2 * PAIR, D), BF16),
-            pltpu.VMEM((2 * PAIR, D), BF16),
-            pltpu.VMEM((NT, ROWS, D), BF16),
-            pltpu.VMEM((NT, ROWS, D), BF16),
-            pltpu.VMEM((NT, 2 * H, ROWS), F32),
-            pltpu.VMEM((NT, 2 * H, ROWS), F32),
+            pltpu.VMEM((BLK, D), BF16),
+            pltpu.VMEM((GROUP, MSG, WIDE), BF16),
+            pltpu.VMEM((GROUP, MSG, WIDE), BF16),
+            pltpu.VMEM((NT, 2, ROWS, WIDE), BF16),
+            pltpu.VMEM((2, 12, ROWS, WIDE), BF16),
+            pltpu.VMEM((2, 4, ROWS, WIDE), BF16),
+            pltpu.VMEM((2, 3, ROWS, WIDE), BF16),
+            pltpu.VMEM((NT, 2, H, ROWS), F32),
+            pltpu.VMEM((2, 12, H, ROWS), F32),
+            pltpu.VMEM((2, 4, H, ROWS), F32),
+            pltpu.VMEM((2, 3, H, ROWS), F32),
             pltpu.VMEM((ROWS, D), F32),
             dma((XSLOTS,)),
-            dma((2 + 3 * GROUP,)),
-            dma((2, NT)),
-            dma((2, NT)),
+            dma((3 + 3 * GROUP,)),
+            dma((GROUP, NT)),
+            dma((GROUP, NT)),
             dma((GROUP, 9)),
             dma((GROUP, 9)),
             dma((GROUP, 7)),
             dma((GROUP, 7)),
+            dma((GROUP, NT)),
+            dma((GROUP, NT)),
             dma((2, NT)),
             dma((2, NT)),
-            dma((NT,)),
-            dma((NT,)),
-            dma((NT,)),
-            dma((NT,)),
-            dma((2,)),
+            dma((2, NT)),
+            dma((2, NT)),
+            dma((2, 4)),
+            dma((2, 4)),
+            dma((2, 4)),
+            dma((2, 4)),
         ],
         compiler_params=pltpu.CompilerParams(
             collective_id=0, has_side_effects=True, vmem_limit_bytes=62 * 2**20
@@ -576,15 +668,15 @@
         ),
     )(
         x_var,
-        var_ids.reshape(VARS, 1),
+        var_ids.reshape(1, VARS),
         var_embed,
-        score_vecs,
+        score_vecs.T,
         v_weight,
         out_weight,
         second_half,
-        norm_gain.reshape(1, D),
-        routes,
-        route_weights,
+        norm_gain,
+        routes.T,
+        route_weights.T,
         w_gate,
         w_up,
         w_down,

time: 124 us -> 90.2 us (0.73)
  the two profiles are of different devices: /device:TPU:36 before, /device:TPU:0 now
where the time goes in v3:
time: 90.2 us; the launch traced here: 90 us
  Pallas kernels  88.3 us (98%)
  local copies, waits for them, and re-layouts  1.67 us (2%)
    pallas_call x1, Pallas kernels, shards(): pl.pallas_call(kernel, out_shape=jax.ShapeDtypeStruct((ROWS, D), BF16), i...  88.3 us

profile of v3, /device:TPU:0, one launch (start us, length us, event | category | flops | bytes accessed | tf_op | source)
XLA Modules:
  0.0 90.0 jit_solution(18306844151821961754)
XLA Ops:
  0.0 88.3 %shard_map.127 = bf16[128,1024]{1,0:T(8,128)(2,1)} custom-call(bf16[3,16,128,1024]{3,2,1,0:T(8,128)(2,1)} %x.1, s32[1,3]{1,0:T(1,128)} %bitcast.7, bf16[48,1024]{1,0:T(8,128)(2,1)} %embed.1, bf16[16,1024]{1,0:T(8,128)(2,1)} %bitcast.4, bf16[1024,1024]{1,0:T(8,128)(2,1)} %vw.1, bf16[1024,1024]{1,0:T(8,128)(2,1)} %ow.1, bf16[128,1024]{1,0:T(8,128)(2,1)} %half.1, ...), custom_call_target="tpu_custom_call" | custom-call | flops 20000000000 | bytes 24000000 | tf_op jit(solution)/shard_map/pallas_call | solution.py:595
  88.3 1.7 %copy.15 = bf16[128,1024]{1,0:T(8,128)(2,1)} copy(bf16[128,1024]{1,0:T(8,128)(2,1)} %shard_map.127) | data formatting | bytes 524288

commit v4 on v3

--- a/solution.py
+++ b/solution.py
@@ -23,6 +23,7 @@
 WIDE = D // 2
 HH = H // 2
 MSG = NT * 16
+MSG_SENT = MSG - 16
 XSLOTS = 3
 
 
@@ -200,21 +201,23 @@
 
     pl.semaphore_wait(barrier, len(greeted))
 
+    def landed(place, sem):
+        pltpu.make_async_copy(place, place, sem).wait()
+
     def msg(i):
         return rows_at(i * 16, 16)
 
     def dispatch(e, o):
         there = (me + o) % NT
-        return remote(pk.at[e, msg(there)], rb.at[e, msg(me)], a_s.at[e, o], a_r.at[e, o], tok_dev(o))
+        return remote(pk.at[e, msg(there)], rb.at[e, msg(me)], a_s.at[e], a_r.at[e], tok_dev(o))
 
     for e in range(GROUP):
         for o in range(1, NT):
             dispatch(e, o).start()
 
     def dispatch_arrived(e):
+        landed(rb.at[e, 0:MSG_SENT], a_r.at[e])
         rb[e, msg(me)] = pk[e, msg(me)]
-        for o in range(1, NT):
-            dispatch(e, o).wait_recv()
 
     msg_half = jnp.right_shift(msg_row, 3) & 1
     for e in range(GROUP):
@@ -236,19 +239,19 @@
     def sum_one(side, dy, dx):
         k = dy * 4 + dx
         if side == 0:
-            slot, dev = (dx - 1) * 4 + dy, along_x(dx)
+            d, first, dev = dy, dx - 1, along_x(dx)
         else:
-            slot, dev = (dy - 1) * 4 + dx, along_y(dy)
+            d, first, dev = dx, dy - 1, along_y(dy)
         return (
-            remote(ns.at[k, side], n1r.at[side, slot], n1_s.at[side, k], n1_r.at[side, k], dev),
-            remote(st_s.at[k, side], st1r.at[side, slot], t1_s.at[side, k], t1_r.at[side, k], dev),
+            remote(ns.at[k, side], n1r.at[side, d, first], n1_s.at[side], n1_r.at[side, d], dev),
+            remote(st_s.at[k, side], st1r.at[side, d, first], t1_s.at[side], t1_r.at[side, d], dev),
         )
 
     def sum_two(side, d):
         dev = along_y(d) if side == 0 else along_x(d)
         return (
-            remote(n2s.at[side, d], n2r.at[side, d - 1], n2_s.at[side, d], n2_r.at[side, d], dev),
-            remote(st2s.at[side, d], st2r.at[side, d - 1], t2_s.at[side, d], t2_r.at[side, d], dev),
+            remote(n2s.at[side, d], n2r.at[side, d - 1], n2_s.at[side], n2_r.at[side], dev),
+            remote(st2s.at[side, d], st2r.at[side, d - 1], t2_s.at[side], t2_r.at[side], dev),
         )
 
     def aggregate(o, _):
@@ -328,23 +331,18 @@
             8: (block_row(core, 2) + low, BLK - low, sib),
         }[kind]
         place = ag.at[e, rows_at(start, size)]
-        return remote(place, place, g_s.at[e, kind], g_r.at[e, kind], dev)
+        return remote(place, place, g_s.at[e], g_r.at[e, min(kind, 4)], dev)
 
     def gather_recv(e, kind):
         low = low_rows(e)
-        start, size, dev = {
-            0: (block_row(core, NZ - 1), BLK, down),
-            1: (block_row(core, 1), BLK, up),
-            2: (block_row(core, 2), low, down),
-            3: (block_row(core, 2) + low, BLK - low, up),
-            4: (block_row(1 - core, 0), BLK, sib),
-            5: (block_row(1 - core, NZ - 1), BLK, sib),
-            6: (block_row(1 - core, 1), BLK, sib),
-            7: (block_row(1 - core, 2), low, sib),
-            8: (block_row(1 - core, 2) + low, BLK - low, sib),
+        start, size = {
+            0: (block_row(core, NZ - 1), BLK),
+            1: (block_row(core, 1), BLK),
+            2: (block_row(core, 2), low),
+            3: (block_row(core, 2) + low, BLK - low),
+            4: ((1 - core) * HALF, HALF),
         }[kind]
-        place = ag.at[e, rows_at(start, size)]
-        remote(place, place, g_s.at[e, kind], g_r.at[e, kind], dev).wait_recv()
+        landed(ag.at[e, rows_at(start, size)], g_r.at[e, kind])
 
     def gather_first(e):
         gather_copy(e, 0).start()
@@ -374,15 +372,14 @@
 
     def sibling_copy(e):
         return remote(
-            pt.at[e, rows_at((1 - core) * HALF, HALF)], sb.at[e], p_s.at[e, 0], p_r.at[e, 0], sib
+            pt.at[e, rows_at((1 - core) * HALF, HALF)], sb.at[e], p_s.at[e], p_r.at[e, 0], sib
         )
 
     def experts_of(e):
         for copy in w_copies[e]:
             copy.wait()
         ffn(e, core * HALF)
-        for kind in range(4, 9):
-            gather_recv(e, kind)
+        gather_recv(e, 4)
         ffn(e, (1 - core) * HALF)
         sibling_copy(e).start()
 
@@ -399,7 +396,7 @@
             5: (part(e, NZ - 1, 0, low), zr2.at[e, 1, 0:low], down),
             6: (part(e, NZ - 1, low, BLK - low), zr2.at[e, 1, low:BLK], down),
         }[kind]
-        return remote(src, dst, p_s.at[e, kind], p_r.at[e, kind], dev)
+        return remote(src, dst, p_s.at[e], p_r.at[e, min(kind, 3)], dev)
 
     def add_sibling(e, dz):
         here = rows_at(block_row(core, dz), BLK)
@@ -407,7 +404,7 @@
         pt[e, here] = (pt[e, here].astype(F32) + sb[e, there].astype(F32)).astype(BF16)
 
     def sum_first(e):
-        sibling_copy(e).wait_recv()
+        landed(sb.at[e], p_r.at[e, 0])
         add_sibling(e, 2)
         sum_step(e, 1).start()
         sum_step(e, 2).start()
@@ -419,18 +416,17 @@
 
     def sum_second(e):
         low = low_rows(e)
-        sum_step(e, 1).wait_recv()
+        landed(zr1.at[e, 0, 0:low], p_r.at[e, 1])
         here = rows_at(block_row(core, 1), low)
         pt[e, here] = (pt[e, here].astype(F32) + zr1[e, 0, 0:low].astype(F32)).astype(BF16)
         sum_step(e, 4).start()
-        sum_step(e, 2).wait_recv()
+        landed(zr1.at[e, 1, 0 : BLK - low], p_r.at[e, 2])
         here = rows_at(block_row(core, NZ - 1) + low, BLK - low)
         pt[e, here] = (pt[e, here].astype(F32) + zr1[e, 1, 0 : BLK - low].astype(F32)).astype(BF16)
         sum_step(e, 6).start()
 
     def sum_third(e):
-        for kind in range(3, 7):
-            sum_step(e, kind).wait_recv()
+        landed(zr2.at[e], p_r.at[e, 3])
         here = rows_at(block_row(core, 0), BLK)
         total = pt[e, here].astype(F32) + zr2[e, 0].astype(F32) + zr2[e, 1].astype(F32)
         so[...] = total.astype(BF16)
@@ -438,7 +434,7 @@
 
     def give_back(e, o):
         there = (me + o) % NT
-        return remote(rs.at[e, msg(there)], rr.at[e, msg(me)], r_s.at[e, o], r_r.at[e, o], tok_dev(o))
+        return remote(rs.at[e, msg(there)], rr.at[e, msg(me)], r_s.at[e], r_r.at[e], tok_dev(o))
 
     def send_back(e):
         place = jnp.where(
@@ -447,7 +443,6 @@
         rs[e] = halves(dot(place, so[...]))
         for o in range(1, NT):
             give_back(e, o).start()
-        rr[e, msg(me)] = rs[e, msg(me)]
 
     def merged(stats, sums):
         peak = stats[0][0:HH]
@@ -468,12 +463,11 @@
         k = d * 4 if side == 0 else d
         stats.append(st_s[k, side])
         sums.append(ns[k, side])
-        for first in range(1, 4):
-            dy, dx = (d, first) if side == 0 else (first, d)
-            for copy in sum_one(side, dy, dx):
-                copy.wait_recv()
-            stats.append(st1r[side, (first - 1) * 4 + d])
-            sums.append(n1r[side, (first - 1) * 4 + d])
+        landed(st1r.at[side, d], t1_r.at[side, d])
+        landed(n1r.at[side, d], n1_r.at[side, d])
+        for first in range(3):
+            stats.append(st1r[side, d, first])
+            sums.append(n1r[side, d, first])
         peak, total, value = merged(stats, sums)
         st2s[side, d, 0:HH] = peak
         st2s[side, d, HH : 2 * HH] = total
@@ -485,9 +479,9 @@
     def merge_two():
         for side in range(2):
             stats, sums = [st2s[side, 0]], [n2s[side, 0]]
+            landed(st2r.at[side], t2_r.at[side])
+            landed(n2r.at[side], n2_r.at[side])
             for d in range(1, 4):
-                for copy in sum_two(side, d):
-                    copy.wait_recv()
                 stats.append(st2r[side, d - 1])
                 sums.append(n2r[side, d - 1])
             acc[:, side * WIDE : (side + 1) * WIDE] = merged(stats, sums)[2]
@@ -495,8 +489,8 @@
         acc[...] = dot(acc[...].astype(BF16), owb[...])
 
     def take_back(e):
-        for o in range(1, NT):
-            give_back(e, o).wait_recv()
+        landed(rr.at[e, 0:MSG_SENT], r_r.at[e])
+        rr[e, msg(me)] = rs[e, msg(me)]
         for side in range(2):
             both = dot(comb[e, side], rr[e])
             acc[:, side * WIDE : (side + 1) * WIDE] += both[0:ROWS] + both[ROWS : 2 * ROWS]
@@ -557,21 +551,15 @@
     out[...] = acc[...].astype(BF16)
 
     for e in range(GROUP):
-        for o in range(1, NT):
-            dispatch(e, o).wait_send()
-            give_back(e, o).wait_send()
-        for kind in range(9):
-            gather_copy(e, kind).wait_send()
-        sibling_copy(e).wait_send()
-        for kind in range(1, 7):
-            sum_step(e, kind).wait_send()
-    for d in range(4):
-        for first in range(1, 4):
-            for copy in sum_one(0, d, first) + sum_one(1, first, d):
-                copy.wait_send()
-        if d > 0:
-            for copy in sum_two(0, d) + sum_two(1, d):
-                copy.wait_send()
+        landed(pk.at[e, 0:MSG_SENT], a_s.at[e])
+        landed(rs.at[e, 0:MSG_SENT], r_s.at[e])
+        landed(ag.at[e, 0 : 7 * BLK], g_s.at[e])
+        landed(pt.at[e, 0 : 7 * BLK], p_s.at[e])
+    for side in range(2):
+        landed(n1r.at[side], n1_s.at[side])
+        landed(st1r.at[side], t1_s.at[side])
+        landed(n2r.at[side], n2_s.at[side])
+        landed(st2r.at[side], t2_s.at[side])
 
 
 def shards(
@@ -633,32 +621,32 @@
             pltpu.VMEM((GROUP, MSG, WIDE), BF16),
             pltpu.VMEM((GROUP, MSG, WIDE), BF16),
             pltpu.VMEM((NT, 2, ROWS, WIDE), BF16),
-            pltpu.VMEM((2, 12, ROWS, WIDE), BF16),
+            pltpu.VMEM((2, 4, 3, ROWS, WIDE), BF16),
             pltpu.VMEM((2, 4, ROWS, WIDE), BF16),
             pltpu.VMEM((2, 3, ROWS, WIDE), BF16),
             pltpu.VMEM((NT, 2, H, ROWS), F32),
-            pltpu.VMEM((2, 12, H, ROWS), F32),
+            pltpu.VMEM((2, 4, 3, H, ROWS), F32),
             pltpu.VMEM((2, 4, H, ROWS), F32),
             pltpu.VMEM((2, 3, H, ROWS), F32),
             pltpu.VMEM((ROWS, D), F32),
             dma((XSLOTS,)),
             dma((3 + 3 * GROUP,)),
-            dma((GROUP, NT)),
-            dma((GROUP, NT)),
-            dma((GROUP, 9)),
-            dma((GROUP, 9)),
-            dma((GROUP, 7)),
-            dma((GROUP, 7)),
-            dma((GROUP, NT)),
-            dma((GROUP, NT)),
-            dma((2, NT)),
-            dma((2, NT)),
-            dma((2, NT)),
-            dma((2, NT)),
+            dma((GROUP,)),
+            dma((GROUP,)),
+            dma((GROUP,)),
+            dma((GROUP, 5)),
+            dma((GROUP,)),
+            dma((GROUP, 4)),
+            dma((GROUP,)),
+            dma((GROUP,)),
+            dma((2,)),
             dma((2, 4)),
+            dma((2,)),
             dma((2, 4)),
-            dma((2, 4)),
-            dma((2, 4)),
+            dma((2,)),
+            dma((2,)),
+            dma((2,)),
+            dma((2,)),
         ],
         compiler_params=pltpu.CompilerParams(
             collective_id=0, has_side_effects=True, vmem_limit_bytes=62 * 2**20

time: 90.2 us -> 85.6 us (0.949)
  Pallas kernels: 88.3 us -> 83.7 us
    pallas_call x1, Pallas kernels: 88.3 us -> 83.7 us  [shards(): pl.pallas_call(kernel, out_shape=jax.ShapeDtypeStruct((ROWS, D), BF16), i...]
where the time goes in v4:
time: 85.6 us; the launch traced here: 85.4 us
  Pallas kernels  83.7 us (98%)
  local copies, waits for them, and re-layouts  1.67 us (2%)
    pallas_call x1, Pallas kernels, shards(): pl.pallas_call(kernel, out_shape=jax.ShapeDtypeStruct((ROWS, D), BF16), i...  83.7 us

profile of v4, /device:TPU:0, one launch (start us, length us, event | category | flops | bytes accessed | tf_op | source)
XLA Modules:
  0.0 85.4 jit_solution(1689096011836607412)
XLA Ops:
  0.0 83.7 %shard_map.127 = bf16[128,1024]{1,0:T(8,128)(2,1)} custom-call(bf16[3,16,128,1024]{3,2,1,0:T(8,128)(2,1)} %x.1, s32[1,3]{1,0:T(1,128)} %bitcast.7, bf16[48,1024]{1,0:T(8,128)(2,1)} %embed.1, bf16[16,1024]{1,0:T(8,128)(2,1)} %bitcast.4, bf16[1024,1024]{1,0:T(8,128)(2,1)} %vw.1, bf16[1024,1024]{1,0:T(8,128)(2,1)} %ow.1, bf16[128,1024]{1,0:T(8,128)(2,1)} %half.1, ...), custom_call_target="tpu_custom_call" | custom-call | flops 20000000000 | bytes 24000000 | tf_op jit(solution)/shard_map/pallas_call | solution.py:583
  83.7 1.7 %copy.15 = bf16[128,1024]{1,0:T(8,128)(2,1)} copy(bf16[128,1024]{1,0:T(8,128)(2,1)} %shard_map.127) | data formatting | bytes 524288

commit v5 on v4

--- a/solution.py
+++ b/solution.py
@@ -25,6 +25,7 @@
 MSG = NT * 16
 MSG_SENT = MSG - 16
 XSLOTS = 3
+FIRST_Z = 3
 
 
 def dot(a, b):
@@ -66,6 +67,8 @@
     comb,
     pk,
     rb,
+    zq,
+    rbq,
     ag,
     pt,
     sb,
@@ -87,6 +90,10 @@
     wsem,
     a_s,
     a_r,
+    q_s,
+    q_r,
+    qx_s,
+    qx_r,
     g_s,
     g_r,
     p_s,
@@ -194,11 +201,13 @@
     def here(e):
         return msg_key == target0 - e * 8, msg_key == target1 - e * 8
 
-    for e in range(GROUP):
+    def pack(e):
         here0, here1 = here(e)
         placing = jnp.where(here0 | here1, 1.0, 0.0).astype(BF16)
         pk[e] = halves(dot(placing, normed))
 
+    pack(FIRST_Z)
+    pack(0)
     pl.semaphore_wait(barrier, len(greeted))
 
     def landed(place, sem):
@@ -211,9 +220,38 @@
         there = (me + o) % NT
         return remote(pk.at[e, msg(there)], rb.at[e, msg(me)], a_s.at[e], a_r.at[e], tok_dev(o))
 
+    def along_z(kind):
+        half_rows = MSG // 2
+        src, dst, dev = {
+            0: (pk.at[FIRST_Z], zq.at[2], up),
+            1: (pk.at[FIRST_Z], zq.at[0], down),
+            2: (zq.at[2, 0:half_rows], zq.at[1, 0:half_rows], up),
+            3: (zq.at[0, half_rows:MSG], zq.at[1, half_rows:MSG], down),
+        }[kind]
+        return remote(src, dst, q_s.at[0], q_r.at[min(kind, 2)], dev)
+
+    def dispatch_z(o):
+        there = (me + o) % NT
+        return remote(zq.at[:, msg(there)], rbq.at[:, msg(me)], qx_s.at[0], qx_r.at[0], tok_dev(o))
+
+    along_z(0).start()
+    along_z(1).start()
     for e in range(GROUP):
+        if 0 < e < FIRST_Z:
+            pack(e)
         for o in range(1, NT):
             dispatch(e, o).start()
+
+    def z_second():
+        landed(zq.at[2], q_r.at[0])
+        along_z(2).start()
+        landed(zq.at[0], q_r.at[1])
+        along_z(3).start()
+
+    def z_third():
+        landed(zq.at[1], q_r.at[2])
+        for o in range(1, NT):
+            dispatch_z(o).start()
 
     def dispatch_arrived(e):
         landed(rb.at[e, 0:MSG_SENT], a_r.at[e])
@@ -304,12 +342,13 @@
     def packed_row(row):
         return jnp.where((row & 7) < CAP, jnp.right_shift(row, 4) * CAP + (row & 7), -1)
 
-    def compact(e):
+    def compact(e, row=mine_ag, source=None):
         col = iota((BLK, MSG), 1)
         match = iota((BLK, MSG), 0) == packed_row(col)
+        rows = rb[e] if source is None else source
         for side in range(2):
             pick = jnp.where(match & ((jnp.right_shift(col, 3) & 1) == side), 1.0, 0.0).astype(BF16)
-            ag[e, rows_at(mine_ag, BLK), side * WIDE : (side + 1) * WIDE] = dot(pick, rb[e]).astype(BF16)
+            ag[e, rows_at(row, BLK), side * WIDE : (side + 1) * WIDE] = dot(pick, rows).astype(BF16)
 
     def low_rows(e):
         return 64 if e % 2 == 0 else 48
@@ -362,6 +401,19 @@
         gather_copy(e, 7).start()
         gather_recv(e, 3)
         gather_copy(e, 8).start()
+
+    def all_copy():
+        place = ag.at[FIRST_Z, rows_at(core * HALF, HALF)]
+        return remote(place, place, g_s.at[FIRST_Z], g_r.at[FIRST_Z, 4], sib)
+
+    def z_arrived():
+        dispatch_arrived(FIRST_Z)
+        compact(FIRST_Z)
+        landed(rbq.at[:, 0:MSG_SENT], qx_r.at[0])
+        rbq[:, msg(me)] = zq[:, msg(me)]
+        for dz in range(1, NZ):
+            compact(FIRST_Z, block_row(core, dz), rbq[dz - 1])
+        all_copy().start()
 
     def ffn(e, start):
         rows = rows_at(start, HALF)
@@ -496,50 +548,47 @@
             acc[:, side * WIDE : (side + 1) * WIDE] += both[0:ROWS] + both[ROWS : 2 * ROWS]
 
     aggregate_range(0, 3)
+    z_second()
     dispatch_arrived(0)
     compact(0)
     gather_first(0)
     dispatch_arrived(1)
     compact(1)
     gather_first(1)
-    aggregate_range(3, 6)
+    aggregate_range(3, 7)
+    z_third()
     dispatch_arrived(2)
     compact(2)
     gather_second(0)
     gather_first(2)
-    aggregate_range(6, 9)
-    dispatch_arrived(3)
-    compact(3)
+    aggregate_range(7, 11)
     gather_second(1)
-    gather_first(3)
     gather_third(0)
-    aggregate_range(9, 10)
+    aggregate_range(11, 12)
     experts_of(0)
-    aggregate_range(10, 12)
+    aggregate_range(12, 14)
     gather_second(2)
     sum_first(0)
     gather_third(1)
     experts_of(1)
-    aggregate_range(12, 14)
-    gather_second(3)
+    aggregate_range(14, 16)
     sum_second(0)
     sum_first(1)
     gather_third(2)
     experts_of(2)
-    aggregate_range(14, 16)
+    for d in range(1, 4):
+        merge_one(0, d)
+        merge_one(1, d)
     sum_third(0)
     sum_second(1)
     sum_first(2)
-    gather_third(3)
+    z_arrived()
     experts_of(3)
-    for d in range(1, 4):
-        merge_one(0, d)
-        merge_one(1, d)
+    merge_one(0, 0)
+    merge_one(1, 0)
     sum_third(1)
     sum_second(2)
     sum_first(3)
-    merge_one(0, 0)
-    merge_one(1, 0)
     sum_third(2)
     sum_second(3)
     merge_two()
@@ -550,10 +599,13 @@
     take_back(3)
     out[...] = acc[...].astype(BF16)
 
+    landed(zq.at[:], q_s.at[0])
+    landed(rbq.at[:, 0:MSG_SENT], qx_s.at[0])
     for e in range(GROUP):
         landed(pk.at[e, 0:MSG_SENT], a_s.at[e])
         landed(rs.at[e, 0:MSG_SENT], r_s.at[e])
-        landed(ag.at[e, 0 : 7 * BLK], g_s.at[e])
+        sent = 4 if e == FIRST_Z else 7
+        landed(ag.at[e, 0 : sent * BLK], g_s.at[e])
         landed(pt.at[e, 0 : 7 * BLK], p_s.at[e])
     for side in range(2):
         landed(n1r.at[side], n1_s.at[side])
@@ -612,6 +664,8 @@
             pltpu.VMEM((GROUP, 2, 2 * ROWS, MSG), BF16),
             pltpu.VMEM((GROUP, MSG, WIDE), BF16),
             pltpu.VMEM((GROUP, MSG, WIDE), BF16),
+            pltpu.VMEM((NZ - 1, MSG, WIDE), BF16),
+            pltpu.VMEM((NZ - 1, MSG, WIDE), BF16),
             pltpu.VMEM((GROUP, 2 * HALF, D), BF16),
             pltpu.VMEM((GROUP, 2 * HALF, D), BF16),
             pltpu.VMEM((GROUP, HALF, D), BF16),
@@ -633,6 +687,10 @@
             dma((3 + 3 * GROUP,)),
             dma((GROUP,)),
             dma((GROUP,)),
+            dma((1,)),
+            dma((3,)),
+            dma((1,)),
+            dma((1,)),
             dma((GROUP,)),
             dma((GROUP, 5)),
             dma((GROUP,)),

time: 85.6 us -> 84.6 us (0.988)
  Pallas kernels: 83.7 us -> 82.8 us
    pallas_call x1, Pallas kernels: 83.7 us -> 82.8 us  [shards(): pl.pallas_call(kernel, out_shape=jax.ShapeDtypeStruct((ROWS, D), BF16), i...]
where the time goes in v5:
time: 84.6 us; the launch traced here: 84.4 us
  Pallas kernels  82.8 us (98%)
  local copies, waits for them, and re-layouts  1.67 us (2%)
    pallas_call x1, Pallas kernels, shards(): pl.pallas_call(kernel, out_shape=jax.ShapeDtypeStruct((ROWS, D), BF16), i...  82.8 us

profile of v5, /device:TPU:0, one launch (start us, length us, event | category | flops | bytes accessed | tf_op | source)
XLA Modules:
  0.0 84.4 jit_solution(17422573275997888496)
XLA Ops:
  0.0 82.8 %shard_map.127 = bf16[128,1024]{1,0:T(8,128)(2,1)} custom-call(bf16[3,16,128,1024]{3,2,1,0:T(8,128)(2,1)} %x.1, s32[1,3]{1,0:T(1,128)} %bitcast.7, bf16[48,1024]{1,0:T(8,128)(2,1)} %embed.1, bf16[16,1024]{1,0:T(8,128)(2,1)} %bitcast.4, bf16[1024,1024]{1,0:T(8,128)(2,1)} %vw.1, bf16[1024,1024]{1,0:T(8,128)(2,1)} %ow.1, bf16[128,1024]{1,0:T(8,128)(2,1)} %half.1, ...), custom_call_target="tpu_custom_call" | custom-call | flops 20000000000 | bytes 24000000 | tf_op jit(solution)/shard_map/pallas_call | solution.py:635
  82.8 1.7 %copy.15 = bf16[128,1024]{1,0:T(8,128)(2,1)} copy(bf16[128,1024]{1,0:T(8,128)(2,1)} %shard_map.127) | data formatting | bytes 524288

commit v6 on v5

--- a/solution.py
+++ b/solution.py
@@ -422,10 +422,13 @@
         hidden = (gate / (1.0 + jnp.exp(-gate)) * both[:, FF : 2 * FF]).astype(BF16)
         pt[e, rows] = dot(hidden, wdn[e]).astype(BF16)
 
-    def sibling_copy(e):
-        return remote(
-            pt.at[e, rows_at((1 - core) * HALF, HALF)], sb.at[e], p_s.at[e], p_r.at[e, 0], sib
-        )
+    def sibling_sem(e, dz):
+        return p_r.at[e, {2: 0, 1: 4, 3: 5, 0: 6}[dz]]
+
+    def sibling_copy(e, dz):
+        src = pt.at[e, rows_at(block_row(1 - core, dz), BLK)]
+        dst = sb.at[e, rows_at(((z + dz) % NZ) * BLK, BLK)]
+        return remote(src, dst, p_s.at[e], sibling_sem(e, dz), sib)
 
     def experts_of(e):
         for copy in w_copies[e]:
@@ -433,7 +436,8 @@
         ffn(e, core * HALF)
         gather_recv(e, 4)
         ffn(e, (1 - core) * HALF)
-        sibling_copy(e).start()
+        for dz in (2, 1, 3, 0):
+            sibling_copy(e, dz).start()
 
     def part(e, dz, start, size):
         return pt.at[e, rows_at(block_row(core, dz) + start, size)]
@@ -453,10 +457,10 @@
     def add_sibling(e, dz):
         here = rows_at(block_row(core, dz), BLK)
         there = rows_at(((z + dz) % NZ) * BLK, BLK)
+        landed(sb.at[e, there], sibling_sem(e, dz))
         pt[e, here] = (pt[e, here].astype(F32) + sb[e, there].astype(F32)).astype(BF16)
 
     def sum_first(e):
-        landed(sb.at[e], p_r.at[e, 0])
         add_sibling(e, 2)
         sum_step(e, 1).start()
         sum_step(e, 2).start()
@@ -694,7 +698,7 @@
             dma((GROUP,)),
             dma((GROUP, 5)),
             dma((GROUP,)),
-            dma((GROUP, 4)),
+            dma((GROUP, 7)),
             dma((GROUP,)),
             dma((GROUP,)),
             dma((2,)),

time: 84.6 us -> 84.7 us (level)
  no operation moved by 1% of the time
where the time goes in v6:
time: 84.7 us; the launch traced here: 84.5 us
  Pallas kernels  82.9 us (98%)
  local copies, waits for them, and re-layouts  1.67 us (2%)
    pallas_call x1, Pallas kernels, shards(): pl.pallas_call(kernel, out_shape=jax.ShapeDtypeStruct((ROWS, D), BF16), i...  82.9 us

profile of v6, /device:TPU:0, one launch (start us, length us, event | category | flops | bytes accessed | tf_op | source)
XLA Modules:
  0.0 84.5 jit_solution(12152957117027394270)
XLA Ops:
  0.0 82.9 %shard_map.127 = bf16[128,1024]{1,0:T(8,128)(2,1)} custom-call(bf16[3,16,128,1024]{3,2,1,0:T(8,128)(2,1)} %x.1, s32[1,3]{1,0:T(1,128)} %bitcast.7, bf16[48,1024]{1,0:T(8,128)(2,1)} %embed.1, bf16[16,1024]{1,0:T(8,128)(2,1)} %bitcast.4, bf16[1024,1024]{1,0:T(8,128)(2,1)} %vw.1, bf16[1024,1024]{1,0:T(8,128)(2,1)} %ow.1, bf16[128,1024]{1,0:T(8,128)(2,1)} %half.1, ...), custom_call_target="tpu_custom_call" | custom-call | flops 20000000000 | bytes 24000000 | tf_op jit(solution)/shard_map/pallas_call | solution.py:639
  82.9 1.7 %copy.15 = bf16[128,1024]{1,0:T(8,128)(2,1)} copy(bf16[128,1024]{1,0:T(8,128)(2,1)} %shard_map.127) | data formatting | bytes 524288
